TPU v7x, 128 devices: a whole 4x4x4 slice. The times are simulated.
128 devices in a mesh: group: 8 (over y, core), tensor: 16 (over z, x).
Axes of the slice: x: 4, y: 4, z: 4, core: 2. Of those that a mesh axis runs over, the one named last changes fastest.
Arguments:
- tokens: bfloat16 [4096, 4096], P('group', 'tensor'), may hold values from -11 to 11
- w_query: bfloat16 [4096, 4096], P(None, 'tensor'), may hold values from -2 to 2
- w_key: bfloat16 [4096, 1024], P(None, 'tensor'), may hold values from -2 to 2
- w_value: bfloat16 [4096, 1024], P(None, 'tensor'), may hold values from -0.09375 to 0.09375
- w_out: bfloat16 [4096, 4096], P('tensor'), may hold values from -0.09375 to 0.09375
- out_grad: bfloat16 [4096, 4096], P('group', 'tensor'), may hold values from -6 to 6
- lengths: int32 [4], replicated, may hold values from 1 to 3584, 4096 in all
- kv_first: int32 [16], replicated, may hold values from 0 to 7, as said below
Outputs:
- mixed: bfloat16 [4096, 4096], P('group', 'tensor')
- tokens_grad: bfloat16 [4096, 4096], P('group', 'tensor')
Inputs may be any that keep to these rules, and one draw needn't show every extreme that they name: kv_first of query block b lies between 0 and b, and for b >= 8 between 0 and b - 8.
All inputs are finite; a program needn't handle non-finite values.
Results may differ from a plain program's by a relative error of at most 0.027.
Values may be sent and summed in bfloat16 or wider, within the bound.
A program may use at most 128 MiB of HBM per device.

v0:
```python
import jax
import jax.numpy as jnp
from jax import lax
from jax.sharding import PartitionSpec as P

HD = 128


def from_partner(value, axis, bit):
    return lax.ppermute(value, axis, [(i, i ^ 1 << bit) for i in range(lax.axis_size(axis))])


def scores_at(query_blk, key_blk, seg_query, seg_key, pos_query, pos_key):
    factor = query_blk.shape[-1] ** (-0.5)
    logits = (
        jnp.einsum("qhd,kd->hqk", query_blk, key_blk, preferred_element_type=jnp.float32) * factor
    )
    visible = (seg_query[:, None] == seg_key[None, :]) & (pos_key[None, :] <= pos_query[:, None])
    return (logits, visible[None, :, :])


def load_block(column, width, keys_all, values_all, segments):
    start = (column * width).astype(jnp.int32)
    key_blk = lax.dynamic_slice_in_dim(keys_all, start, width, 0)
    value_blk = lax.dynamic_slice_in_dim(values_all, start, width, 0)
    seg_key = lax.dynamic_slice_in_dim(segments, start, width, 0)
    return (key_blk, value_blk, seg_key, start + jnp.arange(width, dtype=jnp.int32))


def query_meta(block, width, segments):
    start = block * width
    return (
        lax.dynamic_slice_in_dim(segments, start, width, 0),
        start + jnp.arange(width, dtype=jnp.int32),
    )


def forward_block(query_blk, block, first, keys_all, values_all, segments):
    width = query_blk.shape[0]
    seg_query, pos_query = query_meta(block, width, segments)
    key_blk, value_blk, seg_key, pos_key = load_block(block, width, keys_all, values_all, segments)
    logits, visible = scores_at(query_blk, key_blk, seg_query, seg_key, pos_query, pos_key)
    running = jnp.max(jnp.where(visible, logits, -1e30), axis=-1)

    def first_pass(column, carry):
        peak, total = carry
        key_blk, value_blk, seg_key, pos_key = load_block(
            column, width, keys_all, values_all, segments
        )
        logits, visible = scores_at(query_blk, key_blk, seg_query, seg_key, pos_query, pos_key)
        newpeak = jnp.maximum(peak, jnp.max(jnp.where(visible, logits, -1e30), axis=-1))
        terms = jnp.where(visible, jnp.exp(logits - newpeak[..., None]), 0.0)
        return (newpeak, total * jnp.exp(peak - newpeak) + jnp.sum(terms, axis=-1))

    peak, total = lax.fori_loop(first, block + 1, first_pass, (running, jnp.zeros_like(running)))
    lse = peak + jnp.log(total)

    def second_pass(column, accum):
        key_blk, value_blk, seg_key, pos_key = load_block(
            column, width, keys_all, values_all, segments
        )
        logits, visible = scores_at(query_blk, key_blk, seg_query, seg_key, pos_query, pos_key)
        weights = jnp.where(visible, jnp.exp(logits - lse[..., None]), 0.0).astype(jnp.bfloat16)
        return accum + jnp.einsum(
            "hqk,kd->qhd", weights, value_blk, preferred_element_type=jnp.float32
        )

    start_acc = jnp.zeros(query_blk.shape, jnp.float32)
    accum = lax.fori_loop(first, block + 1, second_pass, start_acc)
    return (accum.astype(jnp.bfloat16), lse)


def backward_block(
    query_blk,
    grad_blk,
    out_blk,
    lse,
    block,
    first,
    keys_all,
    values_all,
    segments,
    key_acc,
    value_acc,
):
    width = query_blk.shape[0]
    factor = query_blk.shape[-1] ** (-0.5)
    seg_query, pos_query = query_meta(block, width, segments)
    delta = jnp.sum(grad_blk.astype(jnp.float32) * out_blk.astype(jnp.float32), axis=-1).T

    def step(column, carry):
        query_grad, key_acc, value_acc = carry
        key_blk, value_blk, seg_key, pos_key = load_block(
            column, width, keys_all, values_all, segments
        )
        logits, visible = scores_at(query_blk, key_blk, seg_query, seg_key, pos_query, pos_key)
        prob = jnp.where(visible, jnp.exp(logits - lse[..., None]), 0.0)
        weights = prob.astype(jnp.bfloat16)
        dprob = jnp.einsum("qhd,kd->hqk", grad_blk, value_blk, preferred_element_type=jnp.float32)
        score_grad = (prob * (dprob - delta[..., None]) * factor).astype(jnp.bfloat16)
        query_grad = query_grad + jnp.einsum(
            "hqk,kd->qhd", score_grad, key_blk, preferred_element_type=jnp.float32
        )
        key_part = jnp.einsum(
            "hqk,qhd->kd", score_grad, query_blk, preferred_element_type=jnp.float32
        )
        value_part = jnp.einsum(
            "hqk,qhd->kd", weights, grad_blk, preferred_element_type=jnp.float32
        )
        start = (column * width).astype(jnp.int32)
        old_key = lax.dynamic_slice_in_dim(key_acc, start, width, 0)
        old_value = lax.dynamic_slice_in_dim(value_acc, start, width, 0)
        key_acc = lax.dynamic_update_slice_in_dim(key_acc, old_key + key_part, start, 0)
        value_acc = lax.dynamic_update_slice_in_dim(value_acc, old_value + value_part, start, 0)
        return (query_grad, key_acc, value_acc)

    start_grad = jnp.zeros(query_blk.shape, jnp.float32)
    return lax.fori_loop(first, block + 1, step, (start_grad, key_acc, value_acc))


def local(tokens, w_query, w_key, w_value, w_out, out_grad, lengths, kv_first):
    tok_rows = tokens.shape[0]
    half = tok_rows // 2
    query_cols = w_query.shape[1]
    pair_cols = w_key.shape[1]
    local_heads = query_cols // HD
    w_inputs = jnp.concatenate([w_query, w_key, w_value], axis=1)
    projected = jnp.dot(
        lax.all_gather(tokens, "tensor", axis=1, tiled=True),
        w_inputs,
        preferred_element_type=jnp.float32,
    ).astype(jnp.bfloat16)
    queries = projected[:, :query_cols]
    key_part = projected[:, query_cols : query_cols + pair_cols]
    value_part = projected[:, query_cols + pair_cols :]
    lower = lax.axis_index("tensor") % 2 == 0
    other_key, other_value = from_partner((key_part, value_part), "tensor", 0)
    key_head = jnp.where(
        lower, jnp.concatenate([key_part, other_key], 1), jnp.concatenate([other_key, key_part], 1)
    )
    value_head = jnp.where(
        lower,
        jnp.concatenate([value_part, other_value], 1),
        jnp.concatenate([other_value, value_part], 1),
    )
    keys_all, values_all = (
        lax.all_gather(key_head, "group", axis=0, tiled=True),
        lax.all_gather(value_head, "group", axis=0, tiled=True),
    )
    tokens_all = keys_all.shape[0]
    positions = jnp.arange(tokens_all, dtype=jnp.int32)
    ends = jnp.cumsum(lengths)
    segments = jnp.sum((positions[:, None] >= ends[None, :]).astype(jnp.int32), axis=1)
    group_index = lax.axis_index("group")
    query_heads = queries.reshape(tok_rows, local_heads, HD)
    first_block = 2 * group_index
    moved = query_heads[half:]
    second_block = 2 * group_index + 1
    out_first, lse_first = forward_block(
        query_heads[:half], first_block, kv_first[first_block], keys_all, values_all, segments
    )
    out_second, lse_second = forward_block(
        moved, second_block, kv_first[second_block], keys_all, values_all, segments
    )
    attended = jnp.concatenate([out_first, out_second], 0).reshape(tok_rows, query_cols)
    w_slice = w_out
    mixed = (
        lax.psum_scatter(
            lax.dot_general(
                w_slice, attended, (((0,), (1,)), ((), ())), preferred_element_type=jnp.float32
            ).astype(jnp.bfloat16),
            "tensor",
            scatter_dimension=0,
            tiled=True,
        )
        .astype(jnp.float32)
        .T.astype(jnp.bfloat16)
    )
    w_slice = w_out
    head_grad = lax.dot_general(
        lax.all_gather(out_grad, "tensor", axis=1, tiled=True),
        w_slice,
        (((1,), (1,)), ((), ())),
        preferred_element_type=jnp.float32,
    ).astype(jnp.bfloat16)
    grad_heads = head_grad.reshape(tok_rows, local_heads, HD)
    grad_second = grad_heads[half:]
    empty_keys = jnp.zeros((tokens_all, HD), jnp.float32)
    dq_first, key_acc, value_acc = backward_block(
        query_heads[:half],
        grad_heads[:half],
        out_first,
        lse_first,
        first_block,
        kv_first[first_block],
        keys_all,
        values_all,
        segments,
        empty_keys,
        empty_keys,
    )
    dq_second, key_acc, value_acc = backward_block(
        moved,
        grad_second,
        out_second,
        lse_second,
        second_block,
        kv_first[second_block],
        keys_all,
        values_all,
        segments,
        key_acc,
        value_acc,
    )
    dq_back = dq_second.astype(jnp.bfloat16)
    query_grad = jnp.concatenate([dq_first.astype(jnp.bfloat16), dq_back], 0).reshape(
        tok_rows, query_cols
    )
    own_key, own_value = (
        lax.psum_scatter(
            key_acc.astype(jnp.bfloat16), "group", scatter_dimension=0, tiled=True
        ).astype(jnp.float32),
        lax.psum_scatter(
            value_acc.astype(jnp.bfloat16), "group", scatter_dimension=0, tiled=True
        ).astype(jnp.float32),
    )
    mine_key = jnp.where(lower, own_key[:, :pair_cols], own_key[:, pair_cols:])
    mine_value = jnp.where(lower, own_value[:, :pair_cols], own_value[:, pair_cols:])
    give_key = jnp.where(lower, own_key[:, pair_cols:], own_key[:, :pair_cols])
    give_value = jnp.where(lower, own_value[:, pair_cols:], own_value[:, :pair_cols])
    got_key, got_value = (
        from_partner(give_key.astype(jnp.bfloat16), "tensor", 0).astype(give_key.dtype),
        from_partner(give_value.astype(jnp.bfloat16), "tensor", 0).astype(give_value.dtype),
    )
    key_grad = mine_key + got_key
    value_grad = mine_value + got_value
    grads_all = jnp.concatenate(
        [query_grad, key_grad.astype(jnp.bfloat16), value_grad.astype(jnp.bfloat16)], 1
    )
    w_slice = w_inputs
    tokens_grad = (
        lax.psum_scatter(
            lax.dot_general(
                w_slice, grads_all, (((1,), (1,)), ((), ())), preferred_element_type=jnp.float32
            ).astype(jnp.bfloat16),
            "tensor",
            scatter_dimension=0,
            tiled=True,
        )
        .astype(jnp.float32)
        .T.astype(jnp.bfloat16)
    )
    return (mixed, tokens_grad)


def solution(mesh):
    return jax.shard_map(
        local,
        mesh=mesh,
        in_specs=(
            P("group", "tensor"),
            P(None, "tensor"),
            P(None, "tensor"),
            P(None, "tensor"),
            P("tensor", None),
            P("group", "tensor"),
            P(),
            P(),
        ),
        out_specs=(P("group", "tensor"), P("group", "tensor")),
        check_vma=False,
    )
```

profile of v0, /device:TPU:0, one launch (start us, length us, event | category | flops | bytes accessed | tf_op | source)
XLA Modules:
  0.0 703.4 jit_solution(15651271319337946893)
XLA Ops:
  10.2 2.8 copy.44
  13.1 57.2 %all-gather.5.cloned.1.call-done = bf16[512,4096]{1,0:T(8,128)(2,1)} async-done(((bf16[512,256]{1,0:T(8,128)(2,1)}), bf16[512,4096]{1,0:T(8,128)(2,1)}) %all-gather.5.cloned.1.call-update) | async-done | bytes 4194320 | tf_op jit(solution)/shard_map/all_gather | solution.py:129
  70.3 5.4 fusion.115
  77.6 3.1 collective-permute-done.1
  88.3 41.5 %all-gather.11.cloned.1.call-done = bf16[512,4096]{1,0:T(8,128)(2,1)} async-done(((bf16[512,256]{1,0:T(8,128)(2,1)}), bf16[512,4096]{1,0:T(8,128)(2,1)}) %all-gather.11.cloned.1.call-update) | async-done | bytes 4194320 | tf_op jit(solution)/shard_map/all_gather | solution.py:181
  129.8 3.5 convolution_convert_fusion.3
  136.1 18.6 %all-gather.9.cloned.1.call-done = bf16[4096,128]{0,1:T(8,128)(2,1)} async-done(((bf16[512,128]{0,1:T(8,128)(2,1)}), bf16[4096,128]{0,1:T(8,128)(2,1)}) %all-gather.9.cloned.1.call-update) | async-done | bytes 1048592 | tf_op jit(solution)/shard_map/all_gather | solution.py:147
  154.7 2.3 copy.49
  158.1 3.0 while.80
  161.2 18.9 %all-gather.7.cloned.1.call-done = bf16[4096,128]{0,1:T(8,128)(2,1)} async-done(((bf16[512,128]{0,1:T(8,128)(2,1)}), bf16[4096,128]{0,1:T(8,128)(2,1)}) %all-gather.7.cloned.1.call-update) | async-done | bytes 1048592 | tf_op jit(solution)/shard_map/all_gather | solution.py:148
  180.1 3.2 while.81
  186.1 1.7 while.79
  188.5 2.3 copy.59
  193.8 10.4 %while.82 = (s32[]{:T(128)}, f32[256,2,128]{0,2,1:T(8,128)S(1)}, f32[4096,128]{1,0:T(8,128)}, f32[4096,128]{1,0:T(8,128)}, s32[]{:T(128)}, /*index=5*/bf16[4096,...) while((s32[]{:T(128)}, f32[256,2,128]{0,2,1:T(8,128)S(1)}, ...), condition=%wide.region_19.20_spmd.clone, body=%wide.region_18.19_spmd.clone.sunk | while | flops 169148928 | bytes 4272371 | solution.py:118
  197.6 1.8 fusion.220
  199.4 1.8 fusion.221
  204.2 20.1 %while.83 = (s32[]{:T(128)}, f32[256,2,128]{0,2,1:T(8,128)S(1)}, f32[4096,128]{1,0:T(8,128)}, f32[4096,128]{1,0:T(8,128)}, s32[]{:T(128)}, /*index=5*/bf16[4096,...) while((s32[]{:T(128)}, f32[256,2,128]{0,2,1:T(8,128)S(1)}, ...), condition=%wide.region_22.23_spmd.clone, body=%wide.region_21.22_spmd.clone.sunk | while | flops 169148928 | bytes 4272371 | solution.py:118
  208.0 1.8 fusion.235
  209.8 1.8 fusion.236
  217.7 1.8 fusion.235
  219.5 1.8 fusion.236
  224.3 2.7 convert_element_type.118
  227.1 2.7 convert_element_type.123
  229.9 262.3 %reduce-scatter.7.cloned.1.call-done = bf16[512,128]{1,0:T(8,128)(2,1)} async-done(((bf16[4096,128]{1,0:T(8,128)(2,1)}), bf16[512,128]{1,0:T(8,128)(2,1)}) %reduce-scatter.7.cloned.1.call-update) | async-done | bytes 131088 | tf_op jit(solution)/shard_map/reduce_scatter | solution.py:220
  494.8 30.4 %reduce-scatter.9.cloned.1.call-done = bf16[512,128]{1,0:T(8,128)(2,1)} async-done(((bf16[4096,128]{1,0:T(8,128)(2,1)}), bf16[512,128]{1,0:T(8,128)(2,1)}) %reduce-scatter.9.cloned.1.call-update) | async-done | bytes 131088 | tf_op jit(solution)/shard_map/reduce_scatter | solution.py:223
  526.2 1.7 collective-permute-start.3
  528.2 3.2 collective-permute-done.3
  531.7 6.5 convolution_convert_fusion
  539.2 3.2 fusion.110
  542.5 72.8 %reduce-scatter.11.cloned.1.call-done = bf16[256,512]{1,0:T(8,128)(2,1)} async-done(((bf16[4096,512]{1,0:T(8,128)(2,1)}), bf16[256,512]{1,0:T(8,128)(2,1)}) %reduce-scatter.11.cloned.1.call-update) | async-done | bytes 262160 | tf_op jit(solution)/shard_map/reduce_scatter | solution.py:242
  615.3 1.8 copy.67
  617.0 79.5 %reduce-scatter.5.cloned.1.call-done = bf16[256,512]{0,1:T(8,128)(2,1)} async-done(((bf16[4096,512]{0,1:T(8,128)(2,1)}), bf16[256,512]{0,1:T(8,128)(2,1)}) %reduce-scatter.5.cloned.1.call-update) | async-done | bytes 262160 | tf_op jit(solution)/shard_map/reduce_scatter | solution.py:168
  (136 shorter events, 44.8 us)
Async XLA Ops:
  7.2 122.6 %copy-start = (bf16[256,4096]{1,0:T(8,128)(2,1)S(1)}, bf16[256,4096]{1,0:T(8,128)(2,1)}, u32[]{:S(2)}) copy-start(bf16[256,4096]{1,0:T(8,128)(2,1)} %param.24) | copy-start | bytes 6291460
  7.2 63.1 %all-gather.5.cloned.1.call-start = ((), (), s32[]{:S(2)}) async-start(), calls=%async_computation.4 | async-start | bytes 4456448 | tf_op jit(solution)/shard_map/all_gather | solution.py:129
  7.9 121.9 %all-gather.11.cloned.1.call-start = ((), (), s32[]{:S(2)}) async-start(), calls=%async_computation.8 | async-start | bytes 4456448 | tf_op jit(solution)/shard_map/all_gather | solution.py:181
  8.7 146.1 %all-gather.9.cloned.1.call-start = ((), (), s32[]{:S(2)}) async-start(), calls=%async_computation.6 | async-start | bytes 1179648 | tf_op jit(solution)/shard_map/all_gather | solution.py:147
  10.2 65.5 %copy-start.1 = (bf16[4096,64]{1,0:T(8,128)(2,1)}, bf16[4096,64]{1,0:T(8,128)(2,1)S(1)}, u32[]{:S(2)}) copy-start(bf16[4096,64]{1,0:T(8,128)(2,1)S(1)} %copy.43) | copy-start | bytes 1572868
  13.1 68.4 %copy-start.6 = (s32[16]{0:T(128)S(1)}, s32[16]{0:T(128)}, u32[]{:S(2)}) copy-start(s32[16]{0:T(128)} %param.27) | copy-start | bytes 196
  13.1 71.9 %copy-start.7 = (s32[4]{0:T(128)S(1)}, s32[4]{0:T(128)}, u32[]{:S(2)}) copy-start(s32[4]{0:T(128)} %param.26) | copy-start | bytes 52
  75.7 0.8 copy-start.4
  76.5 4.3 collective-permute-start.1
  81.4 98.7 %all-gather.7.cloned.1.call-start = ((), (), s32[]{:S(2)}) async-start(), calls=%async_computation.5 | async-start | bytes 1179648 | tf_op jit(solution)/shard_map/all_gather | solution.py:148
  86.1 49.2 %collective-permute-start = (bf16[512,64]{0,1:T(8,128)(2,1)S(1)}, bf16[512,64]{0,1:T(8,128)(2,1)S(1)}, u32[]{:S(2)}, u32[]{:S(2)}) collective-permute-start(bf16[512,64]{0,1:T(8,128)(2,1)S(1)} %get-tuple-element.815), channel_id=1, source_target_pairs={{0,1},{1,0},{2,3},{3,2},{4,5},{5,4},{6,7},{7,6},{8,9},{9,8},{10,11... | collective-permute-start | bytes 196616 | tf_op jit(solution)/shard_map/ppermute | solution.py:10
  136.0 356.2 %reduce-scatter.7.cloned.1.call-start = ((), (), s32[]{:S(2)}) async-start(), calls=%async_computation.9 | async-start | bytes 1179648 | tf_op jit(solution)/shard_map/reduce_scatter | solution.py:220
  158.1 22.0 %copy-start.5 = (bf16[256,2,128]{2,1,0:T(2,128)(2,1)S(1)}, bf16[256,2,128]{2,1,0:T(2,128)(2,1)}, u32[]{:S(2)}) copy-start(bf16[256,2,128]{2,1,0:T(2,128)(2,1)} %copy.56) | copy-start | bytes 393220
  227.0 298.2 %reduce-scatter.9.cloned.1.call-start = ((), (), s32[]{:S(2)}) async-start(), calls=%async_computation.10 | async-start | bytes 1179648 | tf_op jit(solution)/shard_map/reduce_scatter | solution.py:223
  229.8 385.5 %reduce-scatter.11.cloned.1.call-start = ((), (), s32[]{:S(2)}) async-start(), calls=%async_computation.11 | async-start | bytes 4456448 | tf_op jit(solution)/shard_map/reduce_scatter | solution.py:242
  493.3 34.7 %collective-permute-start.2 = (bf16[512,64]{1,0:T(8,128)(2,1)S(1)}, bf16[512,64]{1,0:T(8,128)(2,1)S(1)}, u32[]{:S(2)}, u32[]{:S(2)}) collective-permute-start(bf16[512,64]{1,0:T(8,128)(2,1)S(1)} %select_convert_fusion.1), channel_id=1, source_target_pairs={{0,1},{1,0},{2,3},{3,2},{4,5},{5,4},{6,7},{7,6},{8,9},{9,8},{10,11... | collective-permute-start | bytes 196616 | tf_op jit(solution)/shard_map/ppermute | solution.py:10
  526.2 5.2 collective-permute-start.3
  538.2 0.9 copy-start.2
  538.2 1.0 copy-start.3
  538.3 158.3 %reduce-scatter.5.cloned.1.call-start = ((), (), s32[]{:S(2)}) async-start(), calls=%async_computation.7 | async-start | bytes 4456448 | tf_op jit(solution)/shard_map/reduce_scatter | solution.py:168
Sparse Core Ops, SparseCore 0:
  10.1 60.1 all-gather.4
  72.4 57.3 all-gather.10
  132.1 22.6 all-gather.8
  156.9 23.2 all-gather.6
  227.1 265.0 reduce-scatter.6
  494.5 30.6 reduce-scatter.8
  538.4 76.8 reduce-scatter.10
  619.5 76.9 reduce-scatter.4
where the time goes:
time: 710 us; the launch traced here: 703 us
  waiting for transfers between devices  589 us (83%)
  matrix products  48.6 us (7%)
  local copies, waits for them, and re-layouts  20 us (3%)
  between operations  17.2 us (2%)
  other arithmetic  12.7 us (2%)
  loops' own time  9.8 us (1%)
    reduce_scatter x1, waiting for transfers between devices, local(): lax.psum_scatter(key_acc.astype(jnp.bfloat16), 'group', scatter_dimension...  262 us
    reduce_scatter x1, waiting for transfers between devices, local(): lax.psum_scatter(lax.dot_general(w_slice, attended, (((0,), (1,)), ((), (...  79.5 us
    reduce_scatter x1, waiting for transfers between devices, local(): lax.psum_scatter(lax.dot_general(w_slice, grads_all, (((1,), (1,)), ((),...  72.8 us
    all_gather x1, waiting for transfers between devices, local(): lax.all_gather(tokens, 'tensor', axis=1, tiled=True)  57.2 us
    all_gather x1, waiting for transfers between devices, local(): lax.all_gather(out_grad, 'tensor', axis=1, tiled=True)  41.5 us
    reduce_scatter x1, waiting for transfers between devices, local(): lax.psum_scatter(value_acc.astype(jnp.bfloat16), 'group', scatter_dimensi...  30.4 us
    all_gather x1, waiting for transfers between devices, local(): lax.all_gather(value_head, 'group', axis=0, tiled=True)  18.9 us
    all_gather x1, waiting for transfers between devices, local(): lax.all_gather(key_head, 'group', axis=0, tiled=True)  18.6 us
  transfers between devices with their start and end apart: 12, of which 10 were waited for; matrix products, arithmetic and copies ran while one was open for 5% of the time, Pallas kernels for 0%

commit v1 on v0

--- a/solution.py
+++ b/solution.py
@@ -1,9 +1,269 @@
 import jax
 import jax.numpy as jnp
 from jax import lax
+from jax.experimental import pallas as pl
+from jax.experimental.pallas import tpu as pltpu
 from jax.sharding import PartitionSpec as P
 
 HD = 128
+MESH = pl.DeviceIdType.MESH
+F32 = jnp.float32
+BF16 = jnp.bfloat16
+
+
+def dot(a, b, ca=1, cb=0):
+    return lax.dot_general(a, b, (((ca,), (cb,)), ((), ())), preferred_element_type=F32)
+
+
+class Place:
+    def __init__(self):
+        self.g = lax.axis_index("group")
+        self.t = lax.axis_index("tensor")
+        self.y, self.core = self.g // 2, self.g % 2
+        self.z, self.x = self.t // 4, self.t % 4
+
+    def tensor(self, dz, dx):
+        return (self.z + dz) % 4 * 4 + (self.x + dx) % 4
+
+    def at(self, dz=0, dx=0, dy=0, dcore=0):
+        return (
+            (self.y + dy) % 4 * 2 + (self.core + dcore) % 2,
+            self.tensor(dz, dx),
+        )
+
+
+def greet(place):
+    barrier = pltpu.get_barrier_semaphore()
+    others = [place.at(dx=1), place.at(dx=3), place.at(dz=1), place.at(dz=3)]
+    others += [place.at(dy=1), place.at(dy=3), place.at(dcore=1)]
+    for other in others:
+        pl.semaphore_signal(barrier, inc=1, device_id=other, device_id_type=MESH)
+    pl.semaphore_wait(barrier, len(others))
+
+
+class Gather:
+    def __init__(self, place, own, buf, send, recv):
+        self.place, self.own, self.buf, self.send_sems, self.recv_sems = place, own, buf, send, recv
+        self.sent = []
+
+    @staticmethod
+    def slot(h, du, dv):
+        return (dv % 4) * 4 + du % 4 if h == 0 else (du % 4) * 4 + dv % 4
+
+    @staticmethod
+    def rows(h, part):
+        return pl.ds(h * 256, 256) if part is None else pl.ds(h * 256 + part * 128, 128)
+
+    def ref(self, h, du, dv, part):
+        rows = self.rows(h, part)
+        if du % 4 == 0 and dv % 4 == 0:
+            return self.own.at[rows, :]
+        return self.buf.at[self.slot(h, du, dv), rows, :]
+
+    def push(self, h, axis, sign, du, dv, part=None):
+        if axis == 0:
+            tu, tv = du - sign, dv
+        else:
+            tu, tv = du, dv - sign
+        along_x = (axis == 0) == (h == 0)
+        target = self.place.at(dx=sign) if along_x else self.place.at(dz=sign)
+        copy = pltpu.make_async_remote_copy(
+            src_ref=self.ref(h, du, dv, part),
+            dst_ref=self.buf.at[self.slot(h, tu, tv), self.rows(h, part), :],
+            send_sem=self.send_sems.at[len(self.sent)],
+            recv_sem=self.recv_sems.at[h, self.slot(h, tu, tv), part or 0],
+            device_id=target,
+            device_id_type=MESH,
+        )
+        copy.start()
+        self.sent.append(copy)
+
+    def arrive(self, h, du, dv, part=None):
+        ref = self.buf.at[self.slot(h, du, dv), self.rows(h, part), :]
+        pltpu.make_async_remote_copy(
+            src_ref=ref,
+            dst_ref=ref,
+            send_sem=self.send_sems.at[0],
+            recv_sem=self.recv_sems.at[h, self.slot(h, du, dv), part or 0],
+            device_id=self.place.at(dx=1),
+            device_id_type=MESH,
+        ).wait_recv()
+
+    def far(self, h, axis, du, dv, sign):
+        self.push(h, axis, sign, du, dv, 0 if sign == 1 else 1)
+
+    def stage0(self):
+        for h in (0, 1):
+            for s in (1, -1):
+                self.push(h, 0, s, 0, 0)
+        for h in (0, 1):
+            for s in (1, -1):
+                self.push(h, 1, s, 0, 0)
+
+    def stage1(self):
+        for s in (1, -1):
+            for h in (0, 1):
+                self.arrive(h, -s, 0)
+                self.far(h, 0, -s, 0, s)
+                for w in (1, -1):
+                    self.push(h, 1, w, -s, 0)
+        for s in (1, -1):
+            for h in (0, 1):
+                self.arrive(h, 0, -s)
+                self.far(h, 1, 0, -s, s)
+
+    def stage2(self):
+        for h in (0, 1):
+            for part in (0, 1):
+                self.arrive(h, 2, 0, part)
+            for w in (1, -1):
+                self.push(h, 1, w, 2, 0)
+        for s in (1, -1):
+            for w in (1, -1):
+                for h in (0, 1):
+                    self.arrive(h, -s, -w)
+                    self.far(h, 1, -s, -w, w)
+
+    def stage3(self):
+        for w in (1, -1):
+            for h in (0, 1):
+                self.arrive(h, 2, -w)
+                self.far(h, 1, 2, -w, w)
+
+    def stage4(self, du):
+        for h in (0, 1):
+            for part in (0, 1):
+                self.arrive(h, du, 2, part)
+
+    def finish(self):
+        for copy in self.sent:
+            copy.wait_send()
+
+
+GATHER_SEMS = [pltpu.SemaphoreType.DMA((40,)), pltpu.SemaphoreType.DMA((2, 16, 2))]
+
+READY = [
+    [(0, 0)],
+    [(1, 0), (3, 0), (0, 1), (0, 3)],
+    [(2, 0), (1, 1), (1, 3), (3, 1), (3, 3)],
+    [(2, 1), (2, 3)],
+    [(0, 2), (1, 2), (2, 2), (3, 2)],
+]
+
+
+def kernel_one(
+    tok, wq, wk, wv, wo, og, q_out, kv_out, hg_out,
+    xbuf, gbuf, wall, wkt, wvt, wot, acc, hacc, xs, xr, gs, gr, lsem,
+):
+    place = Place()
+    loads = [
+        pltpu.make_async_copy(tok, xbuf.at[0], lsem.at[0]),
+        pltpu.make_async_copy(wk, wkt, lsem.at[1]),
+        pltpu.make_async_copy(wv, wvt, lsem.at[2]),
+        pltpu.make_async_copy(wq, wall.at[:, pl.ds(0, 256)], lsem.at[3]),
+        pltpu.make_async_copy(og, gbuf.at[0], lsem.at[4]),
+        pltpu.make_async_copy(wo, wot, lsem.at[5]),
+    ]
+    for load in loads:
+        load.start()
+    greet(place)
+    xg = Gather(place, tok, xbuf, xs, xr)
+    gg = Gather(place, og, gbuf, gs, gr)
+    xg.stage0()
+    loads[1].wait()
+    loads[2].wait()
+
+    def join(i, _):
+        rows = pl.ds(pl.multiple_of(i * 256, 256), 256)
+        wall[rows, 256:384] = jnp.concatenate([wkt[rows, :], wvt[rows, :]], axis=1)
+        return 0
+
+    lax.fori_loop(0, 16, join, 0)
+    loads[0].wait()
+    loads[3].wait()
+
+    def project(pairs, first=False):
+        for h in (0, 1):
+            rows = pl.ds(h * 256, 256)
+            total = None
+            for du, dv in pairs:
+                slot = Gather.slot(h, du, dv)
+                chunk = place.tensor(slot // 4, slot % 4)
+                depth = pl.ds(pl.multiple_of(chunk * 256, 256), 256)
+                part = dot(xbuf[slot, rows, :], wall[depth, :])
+                total = part if total is None else total + part
+            acc[rows, :] = total if first else acc[rows, :] + total
+
+    def cotangent(pairs, first=False):
+        for h in (0, 1):
+            rows = pl.ds(h * 256, 256)
+            total = None
+            for du, dv in pairs:
+                slot = Gather.slot(h, du, dv)
+                chunk = place.tensor(slot // 4, slot % 4)
+                depth = pl.ds(pl.multiple_of(chunk * 256, 256), 256)
+                part = dot(gbuf[slot, rows, :], wot[:, depth], 1, 1)
+                total = part if total is None else total + part
+            hacc[rows, :] = total if first else hacc[rows, :] + total
+
+    project(READY[0], True)
+    xg.stage1()
+    project(READY[1])
+    xg.stage2()
+    gg.stage0()
+    project(READY[2])
+    xg.stage3()
+    project(READY[3])
+    loads[4].wait()
+    loads[5].wait()
+    cotangent(READY[0], True)
+    for du in range(4):
+        xg.stage4(du)
+    project(READY[4])
+    gg.stage1()
+    q_out[...] = acc[:, 0:256].astype(BF16)
+    kv_out[...] = acc[:, 256:384].astype(BF16)
+    cotangent(READY[1])
+    gg.stage2()
+    cotangent(READY[2])
+    gg.stage3()
+    cotangent(READY[3])
+    for du in range(4):
+        gg.stage4(du)
+    cotangent(READY[4])
+    hg_out[...] = hacc[...].astype(BF16)
+    xg.finish()
+    gg.finish()
+
+
+def gather_project(tokens, w_query, w_key, w_value, w_out, out_grad):
+    return pl.pallas_call(
+        kernel_one,
+        out_shape=(
+            jax.ShapeDtypeStruct((512, 256), BF16),
+            jax.ShapeDtypeStruct((512, 128), BF16),
+            jax.ShapeDtypeStruct((512, 256), BF16),
+        ),
+        in_specs=[pl.BlockSpec(memory_space=pl.ANY)] * 6,
+        out_specs=[pl.BlockSpec(memory_space=pltpu.VMEM)] * 3,
+        scratch_shapes=[
+            pltpu.VMEM((16, 512, 256), BF16),
+            pltpu.VMEM((16, 512, 256), BF16),
+            pltpu.VMEM((4096, 384), BF16),
+            pltpu.VMEM((4096, 64), BF16),
+            pltpu.VMEM((4096, 64), BF16),
+            pltpu.VMEM((256, 4096), BF16),
+            pltpu.VMEM((512, 384), F32),
+            pltpu.VMEM((512, 256), F32),
+            *GATHER_SEMS,
+            *GATHER_SEMS,
+            pltpu.SemaphoreType.DMA((6,)),
+        ],
+        compiler_params=pltpu.CompilerParams(
+            collective_id=0, has_side_effects=True, vmem_limit_bytes=40 * 1024 * 1024
+        ),
+        name="gather_project",
+    )(tokens, w_query, w_key, w_value, w_out, out_grad)
 
 
 def from_partner(value, axis, bit):
@@ -125,14 +385,9 @@
     pair_cols = w_key.shape[1]
     local_heads = query_cols // HD
     w_inputs = jnp.concatenate([w_query, w_key, w_value], axis=1)
-    projected = jnp.dot(
-        lax.all_gather(tokens, "tensor", axis=1, tiled=True),
-        w_inputs,
-        preferred_element_type=jnp.float32,
-    ).astype(jnp.bfloat16)
-    queries = projected[:, :query_cols]
-    key_part = projected[:, query_cols : query_cols + pair_cols]
-    value_part = projected[:, query_cols + pair_cols :]
+    queries, kv_half, head_grad = gather_project(tokens, w_query, w_key, w_value, w_out, out_grad)
+    key_part = kv_half[:, :pair_cols]
+    value_part = kv_half[:, pair_cols:]
     lower = lax.axis_index("tensor") % 2 == 0
     other_key, other_value = from_partner((key_part, value_part), "tensor", 0)
     key_head = jnp.where(
@@ -176,13 +431,6 @@
         .astype(jnp.float32)
         .T.astype(jnp.bfloat16)
     )
-    w_slice = w_out
-    head_grad = lax.dot_general(
-        lax.all_gather(out_grad, "tensor", axis=1, tiled=True),
-        w_slice,
-        (((1,), (1,)), ((), ())),
-        preferred_element_type=jnp.float32,
-    ).astype(jnp.bfloat16)
     grad_heads = head_grad.reshape(tok_rows, local_heads, HD)
     grad_second = grad_heads[half:]
     empty_keys = jnp.zeros((tokens_all, HD), jnp.float32)

time: 710 us -> 870 us (1.23)
  waiting for transfers between devices: 589 us -> 677 us
  Pallas kernels: 0 us -> 56.7 us
  local copies, waits for them, and re-layouts: 20 us -> 37.5 us
  matrix products: 48.6 us -> 32.5 us
  other arithmetic: 12.7 us -> 27 us
    reduce_scatter x1, waiting for transfers between devices: 30.4 us -> 469 us  [local(): lax.psum_scatter(value_acc.astype(jnp.bfloat16), 'group', scatter_dimensi...]
    reduce_scatter x1, waiting for transfers between devices: 262 us -> 30.3 us  [local(): lax.psum_scatter(key_acc.astype(jnp.bfloat16), 'group', scatter_dimension...]
    all_gather x2 -> x0, waiting for transfers between devices: 98.7 us -> none  [the longest x1 57.2 us: local(): lax.all_gather(tokens, 'tensor', axis=1, tiled=True)]
    pallas_call x0 -> x1, Pallas kernels: none -> 56.7 us  [gather_project(): pl.pallas_call(kernel_one, out_shape=(jax.ShapeDtypeStruct((512, 256), BF...]
    all_gather x1, waiting for transfers between devices: 18.6 us -> 5.2 us  [local(): lax.all_gather(key_head, 'group', axis=0, tiled=True)]
    dot_general x2 -> x0, matrix products: 8.84 us -> none  [the longest x1 5.37 us: local(): jnp.dot(lax.all_gather(tokens, 'tensor', axis=1, tiled=True), w_inputs, p...]
  transfers between devices with their start and end apart: 12 -> 10, of which waited for: 10 -> 8; matrix products, arithmetic and copies ran while one was open for 5% -> 4% of each run, Pallas kernels for 0% -> 0%
where the time goes in v1:
time: 870 us; the launch traced here: 859 us
  waiting for transfers between devices  677 us (78%)
  Pallas kernels  56.7 us (7%)
  local copies, waits for them, and re-layouts  37.5 us (4%)
  matrix products  32.5 us (4%)
  other arithmetic  27 us (3%)
  between operations  16.7 us (2%)
    reduce_scatter x1, waiting for transfers between devices, local(): lax.psum_scatter(value_acc.astype(jnp.bfloat16), 'group', scatter_dimensi...  469 us
    reduce_scatter x1, waiting for transfers between devices, local(): lax.psum_scatter(lax.dot_general(w_slice, attended, (((0,), (1,)), ((), (...  79.4 us
    reduce_scatter x1, waiting for transfers between devices, local(): lax.psum_scatter(lax.dot_general(w_slice, grads_all, (((1,), (1,)), ((),...  72.6 us
    pallas_call x1, Pallas kernels, gather_project(): pl.pallas_call(kernel_one, out_shape=(jax.ShapeDtypeStruct((512, 256), BF...  56.7 us
    reduce_scatter x1, waiting for transfers between devices, local(): lax.psum_scatter(key_acc.astype(jnp.bfloat16), 'group', scatter_dimension...  30.3 us
  transfers between devices with their start and end apart: 10, of which 8 were waited for; matrix products, arithmetic and copies ran while one was open for 4% of the time, Pallas kernels for 0%

profile of v1, /device:TPU:0, one launch (start us, length us, event | category | flops | bytes accessed | tf_op | source)
XLA Modules:
  0.0 859.3 jit_solution(10932778902358511534)
XLA Ops:
  8.9 2.4 copy.38.wv
  16.0 56.7 %gather_project.1 = (bf16[512,256]{1,0:T(8,128)(2,1)S(1)}, bf16[512,128]{1,0:T(8,128)(2,1)S(1)}, bf16[512,256]{1,0:T(8,128)(2,1)S(1)}) custom-call(bf16[512,256]{1,0:T(8,128)(2,1)S(1)} %copy-done.4, bf16[4096,256]{1,0:T(8,128)(2,1)S(1)} %copy-done.2, bf16[4096,64]{1,0:T(8,128)(2,1)S(1)} %copy.37.wk, bf16[4096,64]{1,0:T(8,128)(2,1)S(1)} %copy-done.1, ...), custom_call_target="tpu_custom_call" | custom-call | tf_op jit(solution)/shard_map/gather_project/pallas_call | solution.py:240
  74.7 3.9 collective-permute-done.1
  78.6 1.8 maximum_select_fusion.1
  82.0 1.7 slice_bitcast_fusion.3
  95.7 1.9 maximum_select_fusion
  97.7 5.2 all-gather.5.cloned.1.call-done
  104.6 3.4 while.80
  109.8 3.5 while.78
  114.6 13.8 %all-gather.3.cloned.1.call-done = bf16[4096,128]{1,0:T(8,128)(2,1)} async-done(((bf16[512,128]{1,0:T(8,128)(2,1)}), bf16[4096,128]{1,0:T(8,128)(2,1)}) %all-gather.3.cloned.1.call-update) | async-done | bytes 1048592 | tf_op jit(solution)/shard_map/all_gather | solution.py:403
  128.4 2.3 copy.41
  131.4 3.8 while.81
  133.0 2.3 fusion.202
  136.6 3.8 while.79
  138.1 2.3 fusion.197
  140.4 1.7 multiply_reduce_fusion.1
  145.7 10.8 %while.82 = (s32[]{:T(128)}, f32[256,2,128]{0,2,1:T(8,128)}, f32[4096,128]{1,0:T(8,128)}, f32[4096,128]{1,0:T(8,128)}, s32[]{:T(128)}, /*index=5*/bf16[4096,128]...) while((s32[]{:T(128)}, f32[256,2,128]{0,2,1:T(8,128)}, ...), condition=%wide.region_19.20_spmd.clone, body=%wide.region_18.19_spmd.clone.sunk | while | flops 169148928 | bytes 6893895 | solution.py:378
  151.7 1.9 fusion.217
  153.6 1.8 fusion.216
  158.8 11.1 %while.83 = (s32[]{:T(128)}, f32[256,2,128]{0,2,1:T(8,128)}, f32[4096,128]{1,0:T(8,128)}, f32[4096,128]{1,0:T(8,128)}, s32[]{:T(128)}, /*index=5*/bf16[4096,128]...) while((s32[]{:T(128)}, f32[256,2,128]{0,2,1:T(8,128)}, ...), condition=%wide.region_22.23_spmd.clone, body=%wide.region_21.22_spmd.clone.sunk | while | flops 169148928 | bytes 6369579 | solution.py:378
  165.1 1.9 fusion.232
  167.0 1.8 fusion.231
  170.0 2.7 convert_element_type.111
  172.7 2.7 convert_element_type.106
  177.3 469.0 %reduce-scatter.9.cloned.1.call-done = bf16[512,128]{1,0:T(8,128)(2,1)} async-done(((bf16[4096,128]{1,0:T(8,128)(2,1)}), bf16[512,128]{1,0:T(8,128)(2,1)}) %reduce-scatter.9.cloned.1.call-update) | async-done | bytes 131088 | tf_op jit(solution)/shard_map/reduce_scatter | solution.py:471
  648.9 30.3 %reduce-scatter.7.cloned.1.call-done = bf16[512,128]{1,0:T(8,128)(2,1)} async-done(((bf16[4096,128]{1,0:T(8,128)(2,1)}), bf16[512,128]{1,0:T(8,128)(2,1)}) %reduce-scatter.7.cloned.1.call-update) | async-done | bytes 131088 | tf_op jit(solution)/shard_map/reduce_scatter | solution.py:468
  684.2 2.7 collective-permute-done.2
  688.2 6.2 convolution_convert_fusion
  695.4 3.3 fusion.110
  698.7 72.6 %reduce-scatter.11.cloned.1.call-done = bf16[256,512]{1,0:T(8,128)(2,1)} async-done(((bf16[4096,512]{1,0:T(8,128)(2,1)}), bf16[256,512]{1,0:T(8,128)(2,1)}) %reduce-scatter.11.cloned.1.call-update) | async-done | bytes 262160 | tf_op jit(solution)/shard_map/reduce_scatter | solution.py:490
  771.3 1.8 copy.55
  773.1 79.4 %reduce-scatter.5.cloned.1.call-done = bf16[256,512]{0,1:T(8,128)(2,1)} async-done(((bf16[4096,512]{0,1:T(8,128)(2,1)}), bf16[256,512]{0,1:T(8,128)(2,1)}) %reduce-scatter.5.cloned.1.call-update) | async-done | bytes 262160 | tf_op jit(solution)/shard_map/reduce_scatter | solution.py:423
  (137 shorter events, 62.6 us)
Async XLA Ops:
  7.2 4.1 copy-start
  7.2 95.7 %all-gather.5.cloned.1.call-start = ((), (), s32[]{:S(2)}) async-start(), calls=%async_computation.5 | async-start | bytes 1179648 | tf_op jit(solution)/shard_map/all_gather | solution.py:402
  11.3 1.2 copy-start.1
  12.5 1.6 copy-start.2
  14.1 0.9 copy-start.4
  15.0 0.9 copy-start.5
  16.0 65.7 %copy-start.21 = (s32[4]{0:T(128)S(1)}, s32[4]{0:T(128)}, u32[]{:S(2)}) copy-start(s32[4]{0:T(128)} %param.26) | copy-start | bytes 52
  72.7 0.8 copy-start.3
  72.7 13.5 %copy-start.20 = (s32[16]{0:T(128)S(1)}, s32[16]{0:T(128)}, u32[]{:S(2)}) copy-start(s32[16]{0:T(128)} %param.27) | copy-start | bytes 196
  73.5 5.1 collective-permute-start.1
  80.4 48.1 %all-gather.3.cloned.1.call-start = ((), (), s32[]{:S(2)}) async-start(), calls=%async_computation.4 | async-start | bytes 1179648 | tf_op jit(solution)/shard_map/all_gather | solution.py:403
  80.4 15.3 %collective-permute-start = (bf16[512,64]{1,0:T(8,128)(2,1)}, bf16[512,64]{1,0:T(8,128)(2,1)}, u32[]{:S(2)}, u32[]{:S(2)}) collective-permute-start(bf16[512,64]{1,0:T(8,128)(2,1)} %get-tuple-element.827), channel_id=1, source_target_pairs={{0,1},{1,0},{2,3},{3,2},{4,5},{5,4},{6,7},{7,6},{8,9},{9,8},{10,11... | collective-permute-start | bytes 196616 | tf_op jit(solution)/shard_map/ppermute | solution.py:270
  82.0 3.3 copy-start.17
  83.8 1.5 copy-start.15
  83.8 1.5 copy-start.16
  97.6 548.6 %reduce-scatter.9.cloned.1.call-start = ((), (), s32[]{:S(2)}) async-start(), calls=%async_computation.8 | async-start | bytes 1179648 | tf_op jit(solution)/shard_map/reduce_scatter | solution.py:471
  131.4 3.8 copy-start.18
  145.7 13.2 %copy-start.19 = (f32[2,256]{1,0:T(2,128)S(1)}, f32[2,256]{1,0:T(2,128)}, u32[]{:S(2)}) copy-start(f32[2,256]{1,0:T(2,128)} %get-tuple-element.1591) | copy-start | bytes 6148
  147.4 3.2 copy-start.10
  147.4 6.2 copy-start.6
  151.7 3.6 copy-start.11
  160.9 3.2 copy-start.7
  165.1 3.6 copy-start.8
  172.7 506.5 %reduce-scatter.7.cloned.1.call-start = ((), (), s32[]{:S(2)}) async-start(), calls=%async_computation.7 | async-start | bytes 1179648 | tf_op jit(solution)/shard_map/reduce_scatter | solution.py:468
  172.7 2.8 copy-start.9
  175.5 595.8 %reduce-scatter.11.cloned.1.call-start = ((), (), s32[]{:S(2)}) async-start(), calls=%async_computation.9 | async-start | bytes 4456448 | tf_op jit(solution)/shard_map/reduce_scatter | solution.py:490
  647.3 35.8 %collective-permute-start.3 = (bf16[512,64]{1,0:T(8,128)(2,1)S(1)}, bf16[512,64]{1,0:T(8,128)(2,1)}, u32[]{:S(2)}, u32[]{:S(2)}) collective-permute-start(bf16[512,64]{1,0:T(8,128)(2,1)S(1)} %select_convert_fusion), channel_id=1, source_target_pairs={{0,1},{1,0},{2,3},{3,2},{4,5},{5,4},{6,7},{7,6},{8,9},{9,8},{10,11... | collective-permute-start | bytes 196616 | tf_op jit(solution)/shard_map/ppermute | solution.py:270
  680.1 0.7 copy-start.12
  681.6 5.3 collective-permute-start.2
  694.4 0.9 copy-start.13
  694.4 1.0 copy-start.14
  694.4 158.1 %reduce-scatter.5.cloned.1.call-start = ((), (), s32[]{:S(2)}) async-start(), calls=%async_computation.6 | async-start | bytes 4456448 | tf_op jit(solution)/shard_map/reduce_scatter | solution.py:423
Sparse Core Ops, SparseCore 0:
  80.5 22.3 all-gather.4
  105.2 23.2 all-gather.2
  172.8 473.4 reduce-scatter.8
  648.5 30.6 reduce-scatter.6
  694.5 76.7 reduce-scatter.10
  775.4 77.0 reduce-scatter.4

commit v2 on v1

v2 whole, which is shorter than its diff:
```python
import jax
import jax.numpy as jnp
from jax import lax
from jax.experimental import pallas as pl
from jax.experimental.pallas import tpu as pltpu
from jax.sharding import PartitionSpec as P

HD = 128
LOG2E = 1.4426950408889634
SCALE = HD**-0.5
MESH = pl.DeviceIdType.MESH
F32 = jnp.float32
BF16 = jnp.bfloat16


def dot(a, b, ca=1, cb=0):
    return lax.dot_general(a, b, (((ca,), (cb,)), ((), ())), preferred_element_type=F32)


class Place:
    def __init__(self):
        self.g = lax.axis_index("group")
        self.t = lax.axis_index("tensor")
        self.y, self.core = self.g // 2, self.g % 2
        self.z, self.x = self.t // 4, self.t % 4

    def tensor(self, dz, dx):
        return (self.z + dz) % 4 * 4 + (self.x + dx) % 4

    def at(self, dz=0, dx=0, dy=0, dcore=0):
        return (
            (self.y + dy) % 4 * 2 + (self.core + dcore) % 2,
            self.tensor(dz, dx),
        )


def greet(place):
    barrier = pltpu.get_barrier_semaphore()
    others = [place.at(dx=1), place.at(dx=3), place.at(dz=1), place.at(dz=3)]
    others += [place.at(dy=1), place.at(dy=3), place.at(dcore=1)]
    for other in others:
        pl.semaphore_signal(barrier, inc=1, device_id=other, device_id_type=MESH)
    pl.semaphore_wait(barrier, len(others))


class Gather:
    def __init__(self, place, own, buf, send, recv):
        self.place, self.own, self.buf, self.send_sems, self.recv_sems = place, own, buf, send, recv
        self.sent = []

    @staticmethod
    def slot(h, du, dv):
        return (dv % 4) * 4 + du % 4 if h == 0 else (du % 4) * 4 + dv % 4

    @staticmethod
    def rows(h, part):
        return pl.ds(h * 256, 256) if part is None else pl.ds(h * 256 + part * 128, 128)

    def ref(self, h, du, dv, part):
        rows = self.rows(h, part)
        if du % 4 == 0 and dv % 4 == 0:
            return self.own.at[rows, :]
        return self.buf.at[self.slot(h, du, dv), rows, :]

    def push(self, h, axis, sign, du, dv, part=None):
        if axis == 0:
            tu, tv = du - sign, dv
        else:
            tu, tv = du, dv - sign
        along_x = (axis == 0) == (h == 0)
        target = self.place.at(dx=sign) if along_x else self.place.at(dz=sign)
        copy = pltpu.make_async_remote_copy(
            src_ref=self.ref(h, du, dv, part),
            dst_ref=self.buf.at[self.slot(h, tu, tv), self.rows(h, part), :],
            send_sem=self.send_sems.at[len(self.sent)],
            recv_sem=self.recv_sems.at[h, self.slot(h, tu, tv), part or 0],
            device_id=target,
            device_id_type=MESH,
        )
        copy.start()
        self.sent.append(copy)

    def arrive(self, h, du, dv, part=None):
        ref = self.buf.at[self.slot(h, du, dv), self.rows(h, part), :]
        pltpu.make_async_remote_copy(
            src_ref=ref,
            dst_ref=ref,
            send_sem=self.send_sems.at[0],
            recv_sem=self.recv_sems.at[h, self.slot(h, du, dv), part or 0],
            device_id=self.place.at(dx=1),
            device_id_type=MESH,
        ).wait_recv()

    def far(self, h, axis, du, dv, sign):
        self.push(h, axis, sign, du, dv, 0 if sign == 1 else 1)

    def stage0(self):
        for h in (0, 1):
            for s in (1, -1):
                self.push(h, 0, s, 0, 0)
        for h in (0, 1):
            for s in (1, -1):
                self.push(h, 1, s, 0, 0)

    def stage1(self):
        for s in (1, -1):
            for h in (0, 1):
                self.arrive(h, -s, 0)
                self.far(h, 0, -s, 0, s)
                for w in (1, -1):
                    self.push(h, 1, w, -s, 0)
        for s in (1, -1):
            for h in (0, 1):
                self.arrive(h, 0, -s)
                self.far(h, 1, 0, -s, s)

    def stage2(self):
        for h in (0, 1):
            for part in (0, 1):
                self.arrive(h, 2, 0, part)
            for w in (1, -1):
                self.push(h, 1, w, 2, 0)
        for s in (1, -1):
            for w in (1, -1):
                for h in (0, 1):
                    self.arrive(h, -s, -w)
                    self.far(h, 1, -s, -w, w)

    def stage3(self):
        for w in (1, -1):
            for h in (0, 1):
                self.arrive(h, 2, -w)
                self.far(h, 1, 2, -w, w)

    def stage4(self):
        for du in range(4):
            for h in (0, 1):
                for part in (0, 1):
                    self.arrive(h, du, 2, part)

    def finish(self):
        for copy in self.sent:
            copy.wait_send()


GATHER_SEMS = [pltpu.SemaphoreType.DMA((40,)), pltpu.SemaphoreType.DMA((2, 16, 2))]

READY = [
    [(0, 0)],
    [(1, 0), (3, 0), (0, 1), (0, 3)],
    [(2, 0), (1, 1), (1, 3), (3, 1), (3, 3)],
    [(2, 1), (2, 3)],
    [(0, 2), (1, 2), (2, 2), (3, 2)],
]


class Scatter:
    def __init__(self, place, buf, far, near, send, far_sems, near_sems):
        self.place, self.buf, self.far, self.near = place, buf, far, near
        self.send_sems, self.far_sems, self.near_sems = send, far_sems, near_sems
        self.sent = []

    def where(self, h, line, offset):
        return Gather.slot(h, line, offset) if line < 4 else Gather.slot(h, offset, 0)

    def push(self, h, line, sign, src, dst, sem):
        along_x = (line == 4) == (h == 0)
        target = self.place.at(dx=sign) if along_x else self.place.at(dz=sign)
        copy = pltpu.make_async_remote_copy(
            src_ref=src,
            dst_ref=dst,
            send_sem=self.send_sems.at[len(self.sent)],
            recv_sem=sem,
            device_id=target,
            device_id_type=MESH,
        )
        copy.start()
        self.sent.append(copy)

    def arrive(self, ref, sem):
        pltpu.make_async_remote_copy(
            src_ref=ref,
            dst_ref=ref,
            send_sem=self.send_sems.at[0],
            recv_sem=sem,
            device_id=self.place.at(dx=1),
            device_id_type=MESH,
        ).wait_recv()

    def start(self, h, line):
        slot = self.where(h, line, 2)
        for part, sign in ((0, -1), (1, 1)):
            self.push(
                h, line, sign,
                self.buf.at[slot, Gather.rows(h, part), :],
                self.far.at[h, line, part],
                self.far_sems.at[h, line, part],
            )

    def pass_on(self, h, line):
        for part, sign in ((0, -1), (1, 1)):
            slot = self.where(h, line, sign)
            rows = Gather.rows(h, part)
            self.arrive(self.far.at[h, line, part], self.far_sems.at[h, line, part])
            self.buf[slot, rows, :] = (
                self.buf[slot, rows, :].astype(F32) + self.far[h, line, part].astype(F32)
            ).astype(BF16)
            self.push(
                h, line, sign,
                self.buf.at[slot, Gather.rows(h, None), :],
                self.near.at[h, line, part],
                self.near_sems.at[h, line, part],
            )

    def total(self, h, line):
        for part in (0, 1):
            self.arrive(self.near.at[h, line, part], self.near_sems.at[h, line, part])
        slot = self.where(h, line, 0)
        rows = Gather.rows(h, None)
        value = (
            self.buf[slot, rows, :].astype(F32)
            + self.near[h, line, 0].astype(F32)
            + self.near[h, line, 1].astype(F32)
        ).astype(BF16)
        return slot, rows, value

    def stage0(self):
        for line in (2, 1, 3, 0):
            for h in (0, 1):
                self.start(h, line)

    def stage1(self):
        for line in (2, 1, 3, 0):
            for h in (0, 1):
                self.pass_on(h, line)

    def stage2(self):
        for line in (2, 1, 3, 0):
            for h in (0, 1):
                slot, rows, value = self.total(h, line)
                self.buf[slot, rows, :] = value
                if line == 2:
                    self.start(h, 4)

    def stage3(self):
        for h in (0, 1):
            self.pass_on(h, 4)

    def stage4(self, out):
        for h in (0, 1):
            _, rows, value = self.total(h, 4)
            out[rows, :] = value

    def finish(self):
        for copy in self.sent:
            copy.wait_send()


SCATTER_BUFS = [pltpu.VMEM((2, 5, 2, 128, 256), BF16), pltpu.VMEM((2, 5, 2, 256, 256), BF16)]
SCATTER_SEMS = [
    pltpu.SemaphoreType.DMA((40,)),
    pltpu.SemaphoreType.DMA((2, 5, 2)),
    pltpu.SemaphoreType.DMA((2, 5, 2)),
]


class Links:
    def __init__(self, send, recv):
        self.send_sems, self.recv_sems, self.sent = send, recv, []

    def push(self, index, src, dst, target):
        copy = pltpu.make_async_remote_copy(
            src_ref=src,
            dst_ref=dst,
            send_sem=self.send_sems.at[index],
            recv_sem=self.recv_sems.at[index],
            device_id=target,
            device_id_type=MESH,
        )
        copy.start()
        self.sent.append(copy)

    def arrive(self, index, ref, source):
        pltpu.make_async_remote_copy(
            src_ref=ref,
            dst_ref=ref,
            send_sem=self.send_sems.at[index],
            recv_sem=self.recv_sems.at[index],
            device_id=source,
            device_id_type=MESH,
        ).wait_recv()

    def finish(self):
        for copy in self.sent:
            copy.wait_send()


LINK_SEMS = [pltpu.SemaphoreType.DMA((16,)), pltpu.SemaphoreType.DMA((16,))]


def layer(
    tok, wq, wk, wv, wo, og, lens, firsts, mixed_out, grad_out,
    xbuf, gbuf, wall, wkt, wvt, wot, acc, hacc,
    qs, half_own, half_got, kvall, logits, probs, att, attended_t, linv, dos, dlt, dqt, dkv, dkv16, core_in,
    yfar, ynear, give_buf, got_buf, grads, mfar, mnear, tfar, tnear,
    xs, xr, gs, gr, ms, mfs, mns, ts, tfs, tns, ks, kr, ds_, dr, lsem,
):
    place = Place()
    g, y, core = place.g, place.y, place.core
    loads = [
        pltpu.make_async_copy(tok, xbuf.at[0], lsem.at[0]),
        pltpu.make_async_copy(wk, wkt, lsem.at[1]),
        pltpu.make_async_copy(wv, wvt, lsem.at[2]),
        pltpu.make_async_copy(wq, wall.at[:, pl.ds(0, 256)], lsem.at[3]),
        pltpu.make_async_copy(og, gbuf.at[0], lsem.at[4]),
        pltpu.make_async_copy(wo, wot, lsem.at[5]),
    ]
    for load in loads:
        load.start()
    greet(place)
    xg = Gather(place, tok, xbuf, xs, xr)
    gg = Gather(place, og, gbuf, gs, gr)
    xg.stage0()
    loads[1].wait()
    loads[2].wait()

    def join(i, _):
        rows = pl.ds(pl.multiple_of(i * 256, 256), 256)
        wall[rows, 256:384] = jnp.concatenate([wkt[rows, :], wvt[rows, :]], axis=1)
        dkv[rows, :] = jnp.zeros((256, 256), F32)
        return 0

    lax.fori_loop(0, 16, join, 0)
    loads[0].wait()
    loads[3].wait()

    def span(slot):
        chunk = place.tensor(slot // 4, slot % 4)
        return pl.ds(pl.multiple_of(chunk * 256, 256), 256)

    def project(pairs, first=False):
        for h in (0, 1):
            rows = pl.ds(h * 256, 256)
            total = None
            for du, dv in pairs:
                slot = Gather.slot(h, du, dv)
                part = dot(xbuf[slot, rows, :], wall[span(slot), :])
                total = part if total is None else total + part
            acc[rows, :] = total if first else acc[rows, :] + total

    def cotangent(pairs, first=False):
        for h in (0, 1):
            rows = pl.ds(h * 256, 256)
            total = None
            for du, dv in pairs:
                slot = Gather.slot(h, du, dv)
                part = dot(gbuf[slot, rows, :], wot[:, span(slot)], 1, 1)
                total = part if total is None else total + part
            hacc[rows, :] = total if first else hacc[rows, :] + total

    project(READY[0], True)
    xg.stage1()
    project(READY[1])
    xg.stage2()
    project(READY[2])
    xg.stage3()
    project(READY[3])
    xg.stage4()
    project(READY[4])

    lower = place.t % 2 == 0
    partner = (g, place.t + 1 - 2 * (place.t % 2))
    kv = Links(ks, kr)
    own_half = acc[:, 256:384].astype(BF16)
    half_own[...] = own_half
    kv.push(0, half_own, half_got, partner)
    gg.stage0()
    qs[0] = acc[:, 0:128].astype(BF16)
    qs[1] = acc[:, 128:256].astype(BF16)
    loads[4].wait()
    loads[5].wait()
    cotangent(READY[0], True)
    kv.arrive(0, half_got, partner)
    other_half = half_got[...]
    low = jnp.where(lower, own_half, other_half)
    high = jnp.where(lower, other_half, own_half)
    kvall[g] = jnp.concatenate([low[:, 0:64], high[:, 0:64], low[:, 64:128], high[:, 64:128]], axis=1)

    def group_at(dy, dcore=0):
        return place.at(dy=dy, dcore=dcore)[0]

    sibling = place.at(dcore=1)
    up, down = place.at(dy=1), place.at(dy=3)
    first_rows, last_rows = pl.ds(0, 256), pl.ds(256, 256)
    kv.push(1, kvall.at[g], kvall.at[g], up)
    kv.push(2, kvall.at[g], kvall.at[g], down)
    kv.push(8, kvall.at[g], kvall.at[g], sibling)
    gg.stage1()
    below, above, across = group_at(3), group_at(1), group_at(2)
    kv.arrive(1, kvall.at[below], down)
    kv.push(3, kvall.at[below, first_rows, :], kvall.at[below, first_rows, :], up)
    kv.push(9, kvall.at[below], kvall.at[below], sibling)
    kv.arrive(2, kvall.at[above], up)
    kv.push(4, kvall.at[above, last_rows, :], kvall.at[above, last_rows, :], down)
    kv.push(10, kvall.at[above], kvall.at[above], sibling)
    cotangent(READY[1])
    kv.arrive(3, kvall.at[across, first_rows, :], down)
    kv.arrive(4, kvall.at[across, last_rows, :], up)
    kv.push(11, kvall.at[across], kvall.at[across], sibling)
    for index, dy in ((8, 0), (9, 3), (10, 1), (11, 2)):
        kv.arrive(index, kvall.at[group_at(dy, 1)], sibling)

    lane = lax.broadcasted_iota(jnp.int32, (1, 512), 1)
    position = lane + g * 512
    low_key = jnp.where(lane < 256, firsts[2 * g], firsts[2 * g + 1]) * 256
    end = lens[0]
    for i in range(1, 5):
        low_key = jnp.maximum(low_key, jnp.where(position >= end, end, 0))
        if i < 4:
            end = end + lens[i]
    blocks = 2 * g + 2

    def key_block(c):
        return kvall[c // 2, pl.ds(pl.multiple_of(c % 2 * 256, 256), 256), 0:128]

    def value_block(c):
        return kvall[c // 2, pl.ds(pl.multiple_of(c % 2 * 256, 256), 256), 128:256]

    def forward(h):
        def score(c, peak):
            raw = dot(key_block(c), qs[h], 1, 1) * (SCALE * LOG2E)
            key = lax.broadcasted_iota(jnp.int32, (256, 512), 0) + c * 256
            raw = jnp.where((key >= low_key) & (key <= position), raw, -1e30)
            logits[c] = raw
            return jnp.maximum(peak, jnp.max(raw, axis=0, keepdims=True))

        peak = lax.fori_loop(0, blocks, score, jnp.full((1, 512), -1e30, F32))

        def weigh(c, carry):
            total, out = carry
            prob = jnp.exp2(logits[c] - peak)
            rounded = prob.astype(BF16)
            probs[c, h] = rounded
            return (
                total + jnp.sum(prob, axis=0, keepdims=True),
                out + dot(value_block(c), rounded, 0, 0),
            )

        total, out = lax.fori_loop(
            0, blocks, weigh, (jnp.zeros((1, 512), F32), jnp.zeros((128, 512), F32))
        )
        inverse = 1.0 / total
        linv[h] = inverse
        rounded = (out * inverse).T.astype(BF16)
        attended_t[h] = (out * inverse).astype(BF16)
        att[:, h * 128 : (h + 1) * 128] = rounded

    forward(0)
    gg.stage2()
    cotangent(READY[2])
    forward(1)
    gg.stage3()
    cotangent(READY[3])

    xg.finish()
    early = [s for s in range(16) if s // 4 == 2 or s % 4 == 2]
    late = [s for s in range(16) if s not in early]
    mixed = Scatter(place, xbuf, mfar, mnear, ms, mfs, mns)

    def mix(slots):
        for slot in slots:
            xbuf[slot] = dot(att[...], wot[:, span(slot)]).astype(BF16)

    mix(early)
    gg.stage4()
    mixed.stage0()
    cotangent(READY[4])
    mix(late)

    for h in (0, 1):
        grad_t = hacc[:, h * 128 : (h + 1) * 128].T * linv[h]
        dlt[h] = jnp.sum(grad_t * attended_t[h].astype(F32), axis=0, keepdims=True)
        dos[h] = grad_t.T.astype(BF16)
        dqt[h] = jnp.zeros((128, 512), F32)

    def backward(c, _):
        keys, values = key_block(c), value_block(c)
        rows = pl.ds(pl.multiple_of(c * 256, 256), 256)
        key_part, value_part = None, None
        for h in (0, 1):
            prob = probs[c, h]
            dprob = dot(values, dos[h], 1, 1)
            score = (prob.astype(F32) * (dprob - dlt[h])).astype(BF16)
            dqt[h] += dot(keys, score, 0, 0)
            one, two = dot(score, qs[h]), dot(prob, dos[h])
            key_part = one if h == 0 else key_part + one
            value_part = two if h == 0 else value_part + two
        dkv[rows, 0:128] = key_part * SCALE
        dkv[rows, 128:256] = value_part
        return 0

    def section(i, n):
        lax.fori_loop(blocks * i // n, blocks * (i + 1) // n, backward, 0)

    section(0, 4)
    mixed.stage1()
    section(1, 4)
    section(2, 4)
    mixed.stage2()
    section(3, 4)

    kvg = Links(ds_, dr)

    def narrow(dy, dcore):
        group = group_at(dy, dcore)
        rows = pl.ds(pl.multiple_of(group * 512, 512), 512)
        dkv16[group] = dkv[rows, :].astype(BF16)
        return group

    for dy in (2, 1, 3, 0):
        group = narrow(dy, 1)
        kvg.push(dy, dkv16.at[group], core_in.at[dy], sibling)

    def join_cores(dy):
        group = group_at(dy)
        rows = pl.ds(pl.multiple_of(group * 512, 512), 512)
        kvg.arrive(dy, core_in.at[dy], sibling)
        dkv16[group] = (dkv[rows, :] + core_in[dy].astype(F32)).astype(BF16)
        return group

    group = join_cores(2)
    kvg.push(4, dkv16.at[group, first_rows, :], yfar.at[0], down)
    kvg.push(5, dkv16.at[group, last_rows, :], yfar.at[1], up)
    mixed.stage3()
    group = join_cores(3)
    kvg.arrive(4, yfar.at[0], up)
    dkv16[group, first_rows, :] = (dkv16[group, first_rows, :].astype(F32) + yfar[0].astype(F32)).astype(BF16)
    kvg.push(6, dkv16.at[group], ynear.at[0], down)
    group = join_cores(1)
    kvg.arrive(5, yfar.at[1], down)
    dkv16[group, last_rows, :] = (dkv16[group, last_rows, :].astype(F32) + yfar[1].astype(F32)).astype(BF16)
    kvg.push(7, dkv16.at[group], ynear.at[1], up)
    for h in (0, 1):
        grads[:, h * 128 : (h + 1) * 128] = (dqt[h] * SCALE).T.astype(BF16)
    group = join_cores(0)
    kvg.arrive(6, ynear.at[0], up)
    kvg.arrive(7, ynear.at[1], down)
    summed = dkv16[group].astype(F32) + ynear[0].astype(F32) + ynear[1].astype(F32)
    low = jnp.concatenate([summed[:, 0:64], summed[:, 128:192]], axis=1)
    high = jnp.concatenate([summed[:, 64:128], summed[:, 192:256]], axis=1)
    give_buf[...] = jnp.where(lower, high, low).astype(BF16)
    kvg.push(8, give_buf, got_buf, partner)
    gg.finish()
    mixed.stage4(mixed_out)
    kvg.arrive(8, got_buf, partner)
    grads[:, 256:384] = (jnp.where(lower, low, high) + got_buf[...].astype(F32)).astype(BF16)

    final = Scatter(place, gbuf, tfar, tnear, ts, tfs, tns)

    def spread(slots):
        for slot in slots:
            gbuf[slot] = dot(grads[...], wall[span(slot), :], 1, 1).astype(BF16)

    spread(early)
    final.stage0()
    spread(late)
    final.stage1()
    final.stage2()
    final.stage3()
    final.stage4(grad_out)
    kv.finish()
    kvg.finish()
    mixed.finish()
    final.finish()


def local(*args):
    return tuple(
        pl.pallas_call(
            layer,
            out_shape=(
                jax.ShapeDtypeStruct((512, 256), BF16),
                jax.ShapeDtypeStruct((512, 256), BF16),
            ),
            in_specs=[pl.BlockSpec(memory_space=pl.ANY)] * 6
            + [pl.BlockSpec(memory_space=pltpu.SMEM)] * 2,
            out_specs=[pl.BlockSpec(memory_space=pltpu.VMEM)] * 2,
            scratch_shapes=[
                pltpu.VMEM((16, 512, 256), BF16),
                pltpu.VMEM((16, 512, 256), BF16),
                pltpu.VMEM((4096, 384), BF16),
                pltpu.VMEM((4096, 64), BF16),
                pltpu.VMEM((4096, 64), BF16),
                pltpu.VMEM((256, 4096), BF16),
                pltpu.VMEM((512, 384), F32),
                pltpu.VMEM((512, 256), F32),
                pltpu.VMEM((2, 512, 128), BF16),
                pltpu.VMEM((512, 128), BF16),
                pltpu.VMEM((512, 128), BF16),
                pltpu.VMEM((8, 512, 256), BF16),
                pltpu.VMEM((16, 256, 512), F32),
                pltpu.VMEM((16, 2, 256, 512), BF16),
                pltpu.VMEM((512, 256), BF16),
                pltpu.VMEM((2, 128, 512), BF16),
                pltpu.VMEM((2, 1, 512), F32),
                pltpu.VMEM((2, 512, 128), BF16),
                pltpu.VMEM((2, 1, 512), F32),
                pltpu.VMEM((2, 128, 512), F32),
                pltpu.VMEM((4096, 256), F32),
                pltpu.VMEM((8, 512, 256), BF16),
                pltpu.VMEM((4, 512, 256), BF16),
                pltpu.VMEM((2, 256, 256), BF16),
                pltpu.VMEM((2, 512, 256), BF16),
                pltpu.VMEM((512, 128), BF16),
                pltpu.VMEM((512, 128), BF16),
                pltpu.VMEM((512, 384), BF16),
                *SCATTER_BUFS,
                *SCATTER_BUFS,
                *GATHER_SEMS,
                *GATHER_SEMS,
                *SCATTER_SEMS,
                *SCATTER_SEMS,
                *LINK_SEMS,
                *LINK_SEMS,
                pltpu.SemaphoreType.DMA((6,)),
            ],
            compiler_params=pltpu.CompilerParams(
                collective_id=0, has_side_effects=True, vmem_limit_bytes=60 * 1024 * 1024
            ),
            name="layer",
        )(*args)
    )


def solution(mesh):
    return jax.shard_map(
        local,
        mesh=mesh,
        in_specs=(
            P("group", "tensor"),
            P(None, "tensor"),
            P(None, "tensor"),
            P(None, "tensor"),
            P("tensor", None),
            P("group", "tensor"),
            P(),
            P(),
        ),
        out_specs=(P("group", "tensor"), P("group", "tensor")),
        check_vma=False,
    )
```

time: 870 us -> 148 us (0.17); the launches traced: 859 us -> 147 us
  waiting for transfers between devices: 677 us -> 0 us
  Pallas kernels: 56.7 us -> 139 us
  matrix products: 32.5 us -> 0 us
  local copies, waits for them, and re-layouts: 37.5 us -> 8.13 us
  other arithmetic: 27 us -> 0 us
  between operations: 16.7 us -> 0.64 us
    reduce_scatter x4 -> x0, waiting for transfers between devices: 651 us -> none  [the longest x1 469 us: local(): lax.psum_scatter(value_acc.astype(jnp.bfloat16), 'group', scatter_dimensi...]
    pallas_call x1, Pallas kernels: 56.7 us -> 139 us  [local(): pl.pallas_call(layer, out_shape=(jax.ShapeDtypeStruct((512, 256), BF16),...]
    dot_general x18 -> x0, matrix products: 32.5 us -> none  [the longest x6 6.92 us: scores_at(): jnp.einsum('qhd,kd->hqk', query_blk, key_blk, preferred_element_type=jnp....]
    all_gather x2 -> x0, waiting for transfers between devices: 19 us -> none  [the longest x1 13.8 us: local(): lax.all_gather(value_head, 'group', axis=0, tiled=True)]
    convert_element_type x10 -> x0, other arithmetic: 11.4 us -> none  [the longest x1 2.73 us: local(): key_acc.astype(jnp.bfloat16)]
    unnamed x41 -> x4, local copies, waits for them, and re-layouts: 17 us -> 8.13 us
  transfers between devices with their start and end apart: 10 -> 0, of which waited for: 8 -> 0; matrix products, arithmetic and copies ran while one was open for 4% -> 0% of each run, Pallas kernels for 0% -> 0%
where the time goes in v2:
time: 148 us; the launch traced here: 147 us
  Pallas kernels  139 us (94%)
  local copies, waits for them, and re-layouts  8.13 us (5%)
    pallas_call x1, Pallas kernels, local(): pl.pallas_call(layer, out_shape=(jax.ShapeDtypeStruct((512, 256), BF16),...  139 us
    unnamed x4, local copies, waits for them, and re-layouts  8.13 us

profile of v2, /device:TPU:0, one launch (start us, length us, event | category | flops | bytes accessed | tf_op | source)
XLA Modules:
  0.0 147.4 jit_solution(7355393535853967909)
XLA Ops:
  0.6 2.4 %copy.10.wk = bf16[4096,64]{1,0:T(8,128)(2,1)} copy(bf16[4096,64]{0,1:T(8,128)(2,1)} %param.10) | data formatting | bytes 1048576 | tf_op args[2]
  3.0 2.4 %copy.11.wv = bf16[4096,64]{1,0:T(8,128)(2,1)} copy(bf16[4096,64]{0,1:T(8,128)(2,1)} %param.11) | data formatting | bytes 1048576 | tf_op args[3]
  5.4 138.6 %layer.1 = (bf16[512,256]{1,0:T(8,128)(2,1)}, bf16[512,256]{1,0:T(8,128)(2,1)}) custom-call(bf16[512,256]{1,0:T(8,128)(2,1)} %tok.1, bf16[4096,256]{1,0:T(8,128)(2,1)} %wq.1, bf16[4096,64]{1,0:T(8,128)(2,1)} %copy.10.wk, bf16[4096,64]{1,0:T(8,128)(2,1)} %copy.11.wv, bf16[256,4096]{1,0:T(8,128)(2,1)} %wo.1, bf16[512,256]{1,0:T(8,128)(2,1)} %og.1, s32[4]{0:T(128)} %lens.1, ...), custom_call_target="tpu_custom_call" | custom-call | tf_op jit(solution)/shard_map/layer/pallas_call | solution.py:579
  144.1 1.7 %copy.14 = bf16[512,256]{1,0:T(8,128)(2,1)} copy(bf16[512,256]{1,0:T(8,128)(2,1)} %get-tuple-element.4) | data formatting | bytes 524288
  145.7 1.7 %copy.15 = bf16[512,256]{1,0:T(8,128)(2,1)} copy(bf16[512,256]{1,0:T(8,128)(2,1)} %get-tuple-element.5) | data formatting | bytes 524288

commit v3 on v2

--- a/solution.py
+++ b/solution.py
@@ -298,20 +298,34 @@
 LINK_SEMS = [pltpu.SemaphoreType.DMA((16,)), pltpu.SemaphoreType.DMA((16,))]
 
 
+def each(items, body):
+    def step(i, _):
+        item = items[0]
+        for j in range(1, len(items)):
+            item = jnp.where(i == j, items[j], item)
+        body(item)
+        return 0
+
+    lax.fori_loop(0, len(items), step, 0)
+
+
 def layer(
     tok, wq, wk, wv, wo, og, lens, firsts, mixed_out, grad_out,
-    xbuf, gbuf, wall, wkt, wvt, wot, acc, hacc,
-    qs, half_own, half_got, kvall, logits, probs, att, attended_t, linv, dos, dlt, dqt, dkv, dkv16, core_in,
-    yfar, ynear, give_buf, got_buf, grads, mfar, mnear, tfar, tnear,
-    xs, xr, gs, gr, ms, mfs, mns, ts, tfs, tns, ks, kr, ds_, dr, lsem,
+    xbuf, gbuf, wqt, wkv, wot, acc, kacc, hacc,
+    qs, kvall, logits, probs, peak, sums, outs, att, dos, dlt, dqt, dkv16, core_in,
+    yfar, ynear, grads, mfar, mnear, tfar, tnear,
+    xs, xr, gs, gr, ms, mfs, mns, ts, tfs, tns, ws, wr, ks, kr, ds_, dr, lsem,
 ):
     place = Place()
-    g, y, core = place.g, place.y, place.core
+    g = place.g
+    half = place.t % 2
+    own_rows = pl.ds(pl.multiple_of(half * 64, 64), 64)
+    other_rows = pl.ds(pl.multiple_of((1 - half) * 64, 64), 64)
     loads = [
+        pltpu.make_async_copy(wk, wkv.at[0, own_rows, :], lsem.at[1]),
+        pltpu.make_async_copy(wv, wkv.at[1, own_rows, :], lsem.at[2]),
         pltpu.make_async_copy(tok, xbuf.at[0], lsem.at[0]),
-        pltpu.make_async_copy(wk, wkt, lsem.at[1]),
-        pltpu.make_async_copy(wv, wvt, lsem.at[2]),
-        pltpu.make_async_copy(wq, wall.at[:, pl.ds(0, 256)], lsem.at[3]),
+        pltpu.make_async_copy(wq, wqt, lsem.at[3]),
         pltpu.make_async_copy(og, gbuf.at[0], lsem.at[4]),
         pltpu.make_async_copy(wo, wot, lsem.at[5]),
     ]
@@ -321,94 +335,116 @@
     xg = Gather(place, tok, xbuf, xs, xr)
     gg = Gather(place, og, gbuf, gs, gr)
     xg.stage0()
+
+    def group_at(dy, dcore=0):
+        return place.at(dy=dy, dcore=dcore)[0]
+
+    partner = (g, place.t + 1 - 2 * half)
+    sibling = place.at(dcore=1)
+    up, down = place.at(dy=1), place.at(dy=3)
+    below, above, across = group_at(3), group_at(1), group_at(2)
+    sib_own, sib_below, sib_above, sib_across = (group_at(dy, 1) for dy in (0, 3, 1, 2))
+    first_rows, last_rows = pl.ds(0, 256), pl.ds(256, 256)
+
+    def slice_of(rows, group, kind=None):
+        columns = pl.ds(pl.multiple_of(group * 512, 512), 512)
+        return wkv.at[pl.ds(0, 2) if kind is None else kind, rows, columns]
+
+    wl = Links(ws, wr)
+    loads[0].wait()
     loads[1].wait()
+    wl.push(0, slice_of(own_rows, g), slice_of(own_rows, g), partner)
+
+    def weights_one():
+        ref = slice_of(other_rows, g)
+        wl.arrive(0, ref, partner)
+        wl.push(1, ref, ref, up)
+        wl.push(2, ref, ref, down)
+        wl.push(8, ref, ref, sibling)
+
+    def weights_two():
+        ref = slice_of(other_rows, below)
+        wl.arrive(1, ref, down)
+        wl.push(3, slice_of(other_rows, below, 0), slice_of(other_rows, below, 0), up)
+        wl.push(9, ref, ref, sibling)
+        ref = slice_of(other_rows, above)
+        wl.arrive(2, ref, up)
+        wl.push(4, slice_of(other_rows, above, 1), slice_of(other_rows, above, 1), down)
+        wl.push(10, ref, ref, sibling)
+
+    def weights_three():
+        wl.arrive(3, slice_of(other_rows, across, 0), down)
+        wl.arrive(4, slice_of(other_rows, across, 1), up)
+        ref = slice_of(other_rows, across)
+        wl.push(11, ref, ref, sibling)
+
+    def weights_four():
+        for index, group in ((8, sib_own), (9, sib_below), (10, sib_above), (11, sib_across)):
+            wl.arrive(index, slice_of(other_rows, group), sibling)
+
+    def clear(i, _):
+        dkv16[i] = jnp.zeros((512, 256), BF16)
+        return 0
+
+    lax.fori_loop(0, 8, clear, 0)
     loads[2].wait()
-
-    def join(i, _):
-        rows = pl.ds(pl.multiple_of(i * 256, 256), 256)
-        wall[rows, 256:384] = jnp.concatenate([wkt[rows, :], wvt[rows, :]], axis=1)
-        dkv[rows, :] = jnp.zeros((256, 256), F32)
-        return 0
-
-    lax.fori_loop(0, 16, join, 0)
-    loads[0].wait()
     loads[3].wait()
 
     def span(slot):
         chunk = place.tensor(slot // 4, slot % 4)
         return pl.ds(pl.multiple_of(chunk * 256, 256), 256)
 
-    def project(pairs, first=False):
+    def head_weights(slot):
+        return wkv[:, :, span(slot)].reshape(256, 256)
+
+    def gathered(total_ref, buf, weight, cb, pairs, first=False):
         for h in (0, 1):
             rows = pl.ds(h * 256, 256)
             total = None
             for du, dv in pairs:
                 slot = Gather.slot(h, du, dv)
-                part = dot(xbuf[slot, rows, :], wall[span(slot), :])
+                part = dot(buf[slot, rows, :], weight(slot), 1, cb)
                 total = part if total is None else total + part
-            acc[rows, :] = total if first else acc[rows, :] + total
+            total_ref[rows, :] = total if first else total_ref[rows, :] + total
+
+    def project(pairs, first=False):
+        gathered(acc, xbuf, lambda slot: wqt[span(slot), :], 0, pairs, first)
+
+    def project_kv(pairs, first=False):
+        gathered(kacc, xbuf, head_weights, 1, pairs, first)
 
     def cotangent(pairs, first=False):
-        for h in (0, 1):
-            rows = pl.ds(h * 256, 256)
-            total = None
-            for du, dv in pairs:
-                slot = Gather.slot(h, du, dv)
-                part = dot(gbuf[slot, rows, :], wot[:, span(slot)], 1, 1)
-                total = part if total is None else total + part
-            hacc[rows, :] = total if first else hacc[rows, :] + total
+        gathered(hacc, gbuf, lambda slot: wot[:, span(slot)], 1, pairs, first)
 
     project(READY[0], True)
     xg.stage1()
+    weights_one()
     project(READY[1])
     xg.stage2()
+    weights_two()
+    gg.stage0()
     project(READY[2])
     xg.stage3()
+    weights_three()
     project(READY[3])
+    weights_four()
+    project_kv(READY[0], True)
+    project_kv(READY[1])
+    project_kv(READY[2])
+    project_kv(READY[3])
     xg.stage4()
+    project_kv(READY[4])
+
+    kv = Links(ks, kr)
+    kvall[g] = kacc[...].astype(BF16)
+    kv.push(1, kvall.at[g], kvall.at[g], up)
+    kv.push(2, kvall.at[g], kvall.at[g], down)
+    kv.push(8, kvall.at[g], kvall.at[g], sibling)
     project(READY[4])
-
-    lower = place.t % 2 == 0
-    partner = (g, place.t + 1 - 2 * (place.t % 2))
-    kv = Links(ks, kr)
-    own_half = acc[:, 256:384].astype(BF16)
-    half_own[...] = own_half
-    kv.push(0, half_own, half_got, partner)
-    gg.stage0()
     qs[0] = acc[:, 0:128].astype(BF16)
     qs[1] = acc[:, 128:256].astype(BF16)
     loads[4].wait()
     loads[5].wait()
-    cotangent(READY[0], True)
-    kv.arrive(0, half_got, partner)
-    other_half = half_got[...]
-    low = jnp.where(lower, own_half, other_half)
-    high = jnp.where(lower, other_half, own_half)
-    kvall[g] = jnp.concatenate([low[:, 0:64], high[:, 0:64], low[:, 64:128], high[:, 64:128]], axis=1)
-
-    def group_at(dy, dcore=0):
-        return place.at(dy=dy, dcore=dcore)[0]
-
-    sibling = place.at(dcore=1)
-    up, down = place.at(dy=1), place.at(dy=3)
-    first_rows, last_rows = pl.ds(0, 256), pl.ds(256, 256)
-    kv.push(1, kvall.at[g], kvall.at[g], up)
-    kv.push(2, kvall.at[g], kvall.at[g], down)
-    kv.push(8, kvall.at[g], kvall.at[g], sibling)
-    gg.stage1()
-    below, above, across = group_at(3), group_at(1), group_at(2)
-    kv.arrive(1, kvall.at[below], down)
-    kv.push(3, kvall.at[below, first_rows, :], kvall.at[below, first_rows, :], up)
-    kv.push(9, kvall.at[below], kvall.at[below], sibling)
-    kv.arrive(2, kvall.at[above], up)
-    kv.push(4, kvall.at[above, last_rows, :], kvall.at[above, last_rows, :], down)
-    kv.push(10, kvall.at[above], kvall.at[above], sibling)
-    cotangent(READY[1])
-    kv.arrive(3, kvall.at[across, first_rows, :], down)
-    kv.arrive(4, kvall.at[across, last_rows, :], up)
-    kv.push(11, kvall.at[across], kvall.at[across], sibling)
-    for index, dy in ((8, 0), (9, 3), (10, 1), (11, 2)):
-        kv.arrive(index, kvall.at[group_at(dy, 1)], sibling)
 
     lane = lax.broadcasted_iota(jnp.int32, (1, 512), 1)
     position = lane + g * 512
@@ -418,49 +454,62 @@
         low_key = jnp.maximum(low_key, jnp.where(position >= end, end, 0))
         if i < 4:
             end = end + lens[i]
-    blocks = 2 * g + 2
-
-    def key_block(c):
-        return kvall[c // 2, pl.ds(pl.multiple_of(c % 2 * 256, 256), 256), 0:128]
-
-    def value_block(c):
-        return kvall[c // 2, pl.ds(pl.multiple_of(c % 2 * 256, 256), 256), 128:256]
-
-    def forward(h):
-        def score(c, peak):
-            raw = dot(key_block(c), qs[h], 1, 1) * (SCALE * LOG2E)
-            key = lax.broadcasted_iota(jnp.int32, (256, 512), 0) + c * 256
-            raw = jnp.where((key >= low_key) & (key <= position), raw, -1e30)
-            logits[c] = raw
-            return jnp.maximum(peak, jnp.max(raw, axis=0, keepdims=True))
-
-        peak = lax.fori_loop(0, blocks, score, jnp.full((1, 512), -1e30, F32))
-
-        def weigh(c, carry):
-            total, out = carry
-            prob = jnp.exp2(logits[c] - peak)
+    for h in (0, 1):
+        peak[h] = jnp.full((1, 512), -1e30, F32)
+        sums[h] = jnp.zeros((1, 512), F32)
+        outs[h] = jnp.zeros((128, 512), F32)
+        dqt[h] = jnp.zeros((128, 512), F32)
+
+    def score(k):
+        @pl.when(k <= g)
+        def _():
+            key = lax.broadcasted_iota(jnp.int32, (512, 512), 0) + k * 512
+            visible = (key >= low_key) & (key <= position)
+            for h in (0, 1):
+                raw = dot(kvall[k, :, 0:128], qs[h], 1, 1) * (SCALE * LOG2E)
+                raw = jnp.where(visible, raw, -1e30)
+                logits[k, h] = raw
+                peak[h] = jnp.maximum(peak[h], jnp.max(raw, axis=0, keepdims=True))
+
+    def weigh(k, _):
+        for h in (0, 1):
+            prob = jnp.exp2(logits[k, h] - peak[h])
             rounded = prob.astype(BF16)
-            probs[c, h] = rounded
-            return (
-                total + jnp.sum(prob, axis=0, keepdims=True),
-                out + dot(value_block(c), rounded, 0, 0),
-            )
-
-        total, out = lax.fori_loop(
-            0, blocks, weigh, (jnp.zeros((1, 512), F32), jnp.zeros((128, 512), F32))
-        )
-        inverse = 1.0 / total
-        linv[h] = inverse
-        rounded = (out * inverse).T.astype(BF16)
-        attended_t[h] = (out * inverse).astype(BF16)
-        att[:, h * 128 : (h + 1) * 128] = rounded
-
-    forward(0)
+            probs[k, h] = rounded
+            sums[h] += jnp.sum(prob, axis=0, keepdims=True)
+            outs[h] += dot(kvall[k, :, 128:256], rounded, 0, 0)
+        return 0
+
+    each([g], score)
+    gg.stage1()
+    kv.arrive(1, kvall.at[below], down)
+    kv.push(3, kvall.at[below, first_rows, :], kvall.at[below, first_rows, :], up)
+    kv.push(9, kvall.at[below], kvall.at[below], sibling)
+    kv.arrive(2, kvall.at[above], up)
+    kv.push(4, kvall.at[above, last_rows, :], kvall.at[above, last_rows, :], down)
+    kv.push(10, kvall.at[above], kvall.at[above], sibling)
+    kv.arrive(8, kvall.at[sib_own], sibling)
+    each([sib_own, below, above], score)
+    cotangent(READY[0], True)
+    cotangent(READY[1])
+    kv.arrive(3, kvall.at[across, first_rows, :], down)
+    kv.arrive(4, kvall.at[across, last_rows, :], up)
+    kv.push(11, kvall.at[across], kvall.at[across], sibling)
+    kv.arrive(9, kvall.at[sib_below], sibling)
+    kv.arrive(10, kvall.at[sib_above], sibling)
     gg.stage2()
+    each([sib_below, sib_above, across], score)
     cotangent(READY[2])
-    forward(1)
+    kv.arrive(11, kvall.at[sib_across], sibling)
+    each([sib_across], score)
     gg.stage3()
-    cotangent(READY[3])
+    lax.fori_loop(0, g + 1, weigh, 0)
+
+    for h in (0, 1):
+        inverse = 1.0 / sums[h]
+        sums[h] = inverse
+        outs[h] = outs[h] * inverse
+        att[:, h * 128 : (h + 1) * 128] = outs[h].T.astype(BF16)
 
     xg.finish()
     early = [s for s in range(16) if s // 4 == 2 or s % 4 == 2]
@@ -474,92 +523,84 @@
     mix(early)
     gg.stage4()
     mixed.stage0()
+    cotangent(READY[3])
     cotangent(READY[4])
     mix(late)
 
     for h in (0, 1):
-        grad_t = hacc[:, h * 128 : (h + 1) * 128].T * linv[h]
-        dlt[h] = jnp.sum(grad_t * attended_t[h].astype(F32), axis=0, keepdims=True)
+        grad_t = hacc[:, h * 128 : (h + 1) * 128].T * sums[h]
+        out_t = outs[h].astype(BF16).astype(F32)
+        dlt[h] = jnp.sum(grad_t * out_t, axis=0, keepdims=True)
         dos[h] = grad_t.T.astype(BF16)
-        dqt[h] = jnp.zeros((128, 512), F32)
-
-    def backward(c, _):
-        keys, values = key_block(c), value_block(c)
-        rows = pl.ds(pl.multiple_of(c * 256, 256), 256)
-        key_part, value_part = None, None
-        for h in (0, 1):
-            prob = probs[c, h]
-            dprob = dot(values, dos[h], 1, 1)
-            score = (prob.astype(F32) * (dprob - dlt[h])).astype(BF16)
-            dqt[h] += dot(keys, score, 0, 0)
-            one, two = dot(score, qs[h]), dot(prob, dos[h])
-            key_part = one if h == 0 else key_part + one
-            value_part = two if h == 0 else value_part + two
-        dkv[rows, 0:128] = key_part * SCALE
-        dkv[rows, 128:256] = value_part
-        return 0
-
-    def section(i, n):
-        lax.fori_loop(blocks * i // n, blocks * (i + 1) // n, backward, 0)
-
-    section(0, 4)
+
+    def backward(k):
+        @pl.when(k <= g)
+        def _():
+            keys, values = kvall[k, :, 0:128], kvall[k, :, 128:256]
+            key_part, value_part = None, None
+            for h in (0, 1):
+                prob = probs[k, h]
+                dprob = dot(values, dos[h], 1, 1)
+                grad = (prob.astype(F32) * (dprob - dlt[h])).astype(BF16)
+                dqt[h] += dot(keys, grad, 0, 0)
+                one, two = dot(grad, qs[h]), dot(prob, dos[h])
+                key_part = one if h == 0 else key_part + one
+                value_part = two if h == 0 else value_part + two
+            dkv16[k, :, 0:128] = (key_part * SCALE).astype(BF16)
+            dkv16[k, :, 128:256] = value_part.astype(BF16)
+
+    kvg = Links(ds_, dr)
+
+    def to_sibling(dy, group):
+        kvg.push(dy, dkv16.at[group], core_in.at[dy], sibling)
+
+    def join_cores(dy, group):
+        kvg.arrive(dy, core_in.at[dy], sibling)
+        dkv16[group] = (dkv16[group].astype(F32) + core_in[dy].astype(F32)).astype(BF16)
+
+    def add_far(part, group, rows, source):
+        kvg.arrive(4 + part, yfar.at[part], source)
+        dkv16[group, rows, :] = (dkv16[group, rows, :].astype(F32) + yfar[part].astype(F32)).astype(BF16)
+
+    each([sib_across, across], backward)
+    to_sibling(2, sib_across)
+    join_cores(2, across)
+    kvg.push(4, dkv16.at[across, first_rows, :], yfar.at[0], down)
+    kvg.push(5, dkv16.at[across, last_rows, :], yfar.at[1], up)
     mixed.stage1()
-    section(1, 4)
-    section(2, 4)
+    each([sib_below, sib_above, sib_own], backward)
+    to_sibling(3, sib_below)
+    to_sibling(1, sib_above)
+    to_sibling(0, sib_own)
     mixed.stage2()
-    section(3, 4)
-
-    kvg = Links(ds_, dr)
-
-    def narrow(dy, dcore):
-        group = group_at(dy, dcore)
-        rows = pl.ds(pl.multiple_of(group * 512, 512), 512)
-        dkv16[group] = dkv[rows, :].astype(BF16)
-        return group
-
-    for dy in (2, 1, 3, 0):
-        group = narrow(dy, 1)
-        kvg.push(dy, dkv16.at[group], core_in.at[dy], sibling)
-
-    def join_cores(dy):
-        group = group_at(dy)
-        rows = pl.ds(pl.multiple_of(group * 512, 512), 512)
-        kvg.arrive(dy, core_in.at[dy], sibling)
-        dkv16[group] = (dkv[rows, :] + core_in[dy].astype(F32)).astype(BF16)
-        return group
-
-    group = join_cores(2)
-    kvg.push(4, dkv16.at[group, first_rows, :], yfar.at[0], down)
-    kvg.push(5, dkv16.at[group, last_rows, :], yfar.at[1], up)
+    each([below, above], backward)
     mixed.stage3()
-    group = join_cores(3)
-    kvg.arrive(4, yfar.at[0], up)
-    dkv16[group, first_rows, :] = (dkv16[group, first_rows, :].astype(F32) + yfar[0].astype(F32)).astype(BF16)
-    kvg.push(6, dkv16.at[group], ynear.at[0], down)
-    group = join_cores(1)
-    kvg.arrive(5, yfar.at[1], down)
-    dkv16[group, last_rows, :] = (dkv16[group, last_rows, :].astype(F32) + yfar[1].astype(F32)).astype(BF16)
-    kvg.push(7, dkv16.at[group], ynear.at[1], up)
+    join_cores(3, below)
+    add_far(0, below, first_rows, up)
+    kvg.push(6, dkv16.at[below], ynear.at[0], down)
+    join_cores(1, above)
+    add_far(1, above, last_rows, down)
+    kvg.push(7, dkv16.at[above], ynear.at[1], up)
+    each([g], backward)
     for h in (0, 1):
         grads[:, h * 128 : (h + 1) * 128] = (dqt[h] * SCALE).T.astype(BF16)
-    group = join_cores(0)
+    gg.finish()
+    join_cores(0, g)
+    mixed.stage4(mixed_out)
     kvg.arrive(6, ynear.at[0], up)
     kvg.arrive(7, ynear.at[1], down)
-    summed = dkv16[group].astype(F32) + ynear[0].astype(F32) + ynear[1].astype(F32)
-    low = jnp.concatenate([summed[:, 0:64], summed[:, 128:192]], axis=1)
-    high = jnp.concatenate([summed[:, 64:128], summed[:, 192:256]], axis=1)
-    give_buf[...] = jnp.where(lower, high, low).astype(BF16)
-    kvg.push(8, give_buf, got_buf, partner)
-    gg.finish()
-    mixed.stage4(mixed_out)
-    kvg.arrive(8, got_buf, partner)
-    grads[:, 256:384] = (jnp.where(lower, low, high) + got_buf[...].astype(F32)).astype(BF16)
+    grads[:, 256:512] = (
+        dkv16[g].astype(F32) + ynear[0].astype(F32) + ynear[1].astype(F32)
+    ).astype(BF16)
 
     final = Scatter(place, gbuf, tfar, tnear, ts, tfs, tns)
 
     def spread(slots):
         for slot in slots:
-            gbuf[slot] = dot(grads[...], wall[span(slot), :], 1, 1).astype(BF16)
+            gbuf[slot] = (
+                dot(grads[:, 0:256], wqt[span(slot), :], 1, 1)
+                + dot(grads[:, 256:512], head_weights(slot), 1, 0)
+            ).astype(BF16)
 
     spread(early)
     final.stage0()
@@ -568,13 +609,14 @@
     final.stage2()
     final.stage3()
     final.stage4(grad_out)
+    wl.finish()
     kv.finish()
     kvg.finish()
     mixed.finish()
     final.finish()
 
 
-def local(*args):
+def local(tokens, w_query, w_key, w_value, w_out, out_grad, lengths, kv_first):
     return tuple(
         pl.pallas_call(
             layer,
@@ -588,32 +630,28 @@
             scratch_shapes=[
                 pltpu.VMEM((16, 512, 256), BF16),
                 pltpu.VMEM((16, 512, 256), BF16),
-                pltpu.VMEM((4096, 384), BF16),
-                pltpu.VMEM((4096, 64), BF16),
-                pltpu.VMEM((4096, 64), BF16),
+                pltpu.VMEM((4096, 256), BF16),
+                pltpu.VMEM((2, 128, 4096), BF16),
                 pltpu.VMEM((256, 4096), BF16),
-                pltpu.VMEM((512, 384), F32),
+                pltpu.VMEM((512, 256), F32),
+                pltpu.VMEM((512, 256), F32),
                 pltpu.VMEM((512, 256), F32),
                 pltpu.VMEM((2, 512, 128), BF16),
-                pltpu.VMEM((512, 128), BF16),
-                pltpu.VMEM((512, 128), BF16),
                 pltpu.VMEM((8, 512, 256), BF16),
-                pltpu.VMEM((16, 256, 512), F32),
-                pltpu.VMEM((16, 2, 256, 512), BF16),
+                pltpu.VMEM((8, 2, 512, 512), F32),
+                pltpu.VMEM((8, 2, 512, 512), BF16),
+                pltpu.VMEM((2, 1, 512), F32),
+                pltpu.VMEM((2, 1, 512), F32),
+                pltpu.VMEM((2, 128, 512), F32),
                 pltpu.VMEM((512, 256), BF16),
-                pltpu.VMEM((2, 128, 512), BF16),
-                pltpu.VMEM((2, 1, 512), F32),
                 pltpu.VMEM((2, 512, 128), BF16),
                 pltpu.VMEM((2, 1, 512), F32),
                 pltpu.VMEM((2, 128, 512), F32),
-                pltpu.VMEM((4096, 256), F32),
                 pltpu.VMEM((8, 512, 256), BF16),
                 pltpu.VMEM((4, 512, 256), BF16),
                 pltpu.VMEM((2, 256, 256), BF16),
                 pltpu.VMEM((2, 512, 256), BF16),
-                pltpu.VMEM((512, 128), BF16),
-                pltpu.VMEM((512, 128), BF16),
-                pltpu.VMEM((512, 384), BF16),
+                pltpu.VMEM((512, 512), BF16),
                 *SCATTER_BUFS,
                 *SCATTER_BUFS,
                 *GATHER_SEMS,
@@ -622,13 +660,14 @@
                 *SCATTER_SEMS,
                 *LINK_SEMS,
                 *LINK_SEMS,
+                *LINK_SEMS,
                 pltpu.SemaphoreType.DMA((6,)),
             ],
             compiler_params=pltpu.CompilerParams(
-                collective_id=0, has_side_effects=True, vmem_limit_bytes=60 * 1024 * 1024
+                collective_id=0, has_side_effects=True, vmem_limit_bytes=62 * 1024 * 1024
             ),
             name="layer",
-        )(*args)
+        )(tokens, w_query, w_key.T, w_value.T, w_out, out_grad, lengths, kv_first)
     )
 
 

time: 148 us -> 126 us (0.85)
  Pallas kernels: 139 us -> 122 us
  local copies, waits for them, and re-layouts: 8.13 us -> 3.34 us
    pallas_call x1, Pallas kernels: 139 us -> 122 us  [local(): pl.pallas_call(layer, out_shape=(jax.ShapeDtypeStruct((512, 256), BF16),...]
    unnamed x4 -> x2, local copies, waits for them, and re-layouts: 8.13 us -> 3.34 us
where the time goes in v3:
time: 126 us
  Pallas kernels  122 us (97%)
  local copies, waits for them, and re-layouts  3.34 us (3%)
    pallas_call x1, Pallas kernels, local(): pl.pallas_call(layer, out_shape=(jax.ShapeDtypeStruct((512, 256), BF16),...  122 us
    unnamed x2, local copies, waits for them, and re-layouts  3.34 us

profile of v3, /device:TPU:0, one launch (start us, length us, event | category | flops | bytes accessed | tf_op | source)
XLA Modules:
  0.0 125.7 jit_solution(11835752311249999860)
XLA Ops:
  0.6 121.7 %layer.1 = (bf16[512,256]{1,0:T(8,128)(2,1)}, bf16[512,256]{1,0:T(8,128)(2,1)}) custom-call(bf16[512,256]{1,0:T(8,128)(2,1)} %tok.1, bf16[4096,256]{1,0:T(8,128)(2,1)} %wq.1, bf16[64,4096]{1,0:T(8,128)(2,1)} %bitcast.2, bf16[64,4096]{1,0:T(8,128)(2,1)} %bitcast.3, bf16[256,4096]{1,0:T(8,128)(2,1)} %wo.1, bf16[512,256]{1,0:T(8,128)(2,1)} %og.1, s32[4]{0:T(128)} %lens.1, ...), custom_call_target="tpu_custom_call" | custom-call | tf_op jit(solution)/shard_map/layer/pallas_call | solution.py:621
  122.3 1.7 %copy.12 = bf16[512,256]{1,0:T(8,128)(2,1)} copy(bf16[512,256]{1,0:T(8,128)(2,1)} %get-tuple-element.4) | data formatting | bytes 524288
  124.0 1.7 %copy.13 = bf16[512,256]{1,0:T(8,128)(2,1)} copy(bf16[512,256]{1,0:T(8,128)(2,1)} %get-tuple-element.5) | data formatting | bytes 524288

commit v4 on v3

--- a/solution.py
+++ b/solution.py
@@ -114,12 +114,14 @@
                 self.arrive(h, 0, -s)
                 self.far(h, 1, 0, -s, s)
 
-    def stage2(self):
+    def stage2a(self):
         for h in (0, 1):
             for part in (0, 1):
                 self.arrive(h, 2, 0, part)
             for w in (1, -1):
                 self.push(h, 1, w, 2, 0)
+
+    def stage2b(self):
         for s in (1, -1):
             for w in (1, -1):
                 for h in (0, 1):
@@ -224,29 +226,42 @@
         ).astype(BF16)
         return slot, rows, value
 
-    def stage0(self):
+    def stage0(self, fill):
+        done = []
         for line in (2, 1, 3, 0):
             for h in (0, 1):
+                slot = self.where(h, line, 2)
+                if slot not in done:
+                    fill(slot)
+                    done.append(slot)
                 self.start(h, line)
+        for slot in range(16):
+            if slot not in done:
+                fill(slot)
 
     def stage1(self):
         for line in (2, 1, 3, 0):
             for h in (0, 1):
                 self.pass_on(h, line)
 
+    def settle(self, line):
+        for h in (0, 1):
+            slot, rows, value = self.total(h, line)
+            self.buf[slot, rows, :] = value
+
     def stage2(self):
-        for line in (2, 1, 3, 0):
-            for h in (0, 1):
-                slot, rows, value = self.total(h, line)
-                self.buf[slot, rows, :] = value
-                if line == 2:
-                    self.start(h, 4)
+        self.settle(2)
+        for h in (0, 1):
+            self.start(h, 4)
 
     def stage3(self):
+        self.settle(1)
+        self.settle(3)
         for h in (0, 1):
             self.pass_on(h, 4)
 
     def stage4(self, out):
+        self.settle(0)
         for h in (0, 1):
             _, rows, value = self.total(h, 4)
             out[rows, :] = value
@@ -420,11 +435,12 @@
     xg.stage1()
     weights_one()
     project(READY[1])
-    xg.stage2()
+    xg.stage2a()
+    xg.stage2b()
     weights_two()
-    gg.stage0()
     project(READY[2])
     xg.stage3()
+    gg.stage0()
     weights_three()
     project(READY[3])
     weights_four()
@@ -482,6 +498,9 @@
 
     each([g], score)
     gg.stage1()
+    cotangent(READY[0], True)
+    gg.stage2a()
+    cotangent(READY[1])
     kv.arrive(1, kvall.at[below], down)
     kv.push(3, kvall.at[below, first_rows, :], kvall.at[below, first_rows, :], up)
     kv.push(9, kvall.at[below], kvall.at[below], sibling)
@@ -490,19 +509,16 @@
     kv.push(10, kvall.at[above], kvall.at[above], sibling)
     kv.arrive(8, kvall.at[sib_own], sibling)
     each([sib_own, below, above], score)
-    cotangent(READY[0], True)
-    cotangent(READY[1])
+    gg.stage2b()
     kv.arrive(3, kvall.at[across, first_rows, :], down)
     kv.arrive(4, kvall.at[across, last_rows, :], up)
     kv.push(11, kvall.at[across], kvall.at[across], sibling)
     kv.arrive(9, kvall.at[sib_below], sibling)
     kv.arrive(10, kvall.at[sib_above], sibling)
-    gg.stage2()
     each([sib_below, sib_above, across], score)
-    cotangent(READY[2])
+    gg.stage3()
     kv.arrive(11, kvall.at[sib_across], sibling)
     each([sib_across], score)
-    gg.stage3()
     lax.fori_loop(0, g + 1, weigh, 0)
 
     for h in (0, 1):
@@ -512,20 +528,16 @@
         att[:, h * 128 : (h + 1) * 128] = outs[h].T.astype(BF16)
 
     xg.finish()
-    early = [s for s in range(16) if s // 4 == 2 or s % 4 == 2]
-    late = [s for s in range(16) if s not in early]
     mixed = Scatter(place, xbuf, mfar, mnear, ms, mfs, mns)
 
-    def mix(slots):
-        for slot in slots:
-            xbuf[slot] = dot(att[...], wot[:, span(slot)]).astype(BF16)
-
-    mix(early)
+    def mix(slot):
+        xbuf[slot] = dot(att[...], wot[:, span(slot)]).astype(BF16)
+
+    mixed.stage0(mix)
+    cotangent(READY[2])
+    cotangent(READY[3])
     gg.stage4()
-    mixed.stage0()
-    cotangent(READY[3])
     cotangent(READY[4])
-    mix(late)
 
     for h in (0, 1):
         grad_t = hacc[:, h * 128 : (h + 1) * 128].T * sums[h]
@@ -564,17 +576,16 @@
 
     each([sib_across, across], backward)
     to_sibling(2, sib_across)
+    mixed.stage1()
     join_cores(2, across)
     kvg.push(4, dkv16.at[across, first_rows, :], yfar.at[0], down)
     kvg.push(5, dkv16.at[across, last_rows, :], yfar.at[1], up)
-    mixed.stage1()
     each([sib_below, sib_above, sib_own], backward)
     to_sibling(3, sib_below)
     to_sibling(1, sib_above)
     to_sibling(0, sib_own)
     mixed.stage2()
     each([below, above], backward)
-    mixed.stage3()
     join_cores(3, below)
     add_far(0, below, first_rows, up)
     kvg.push(6, dkv16.at[below], ynear.at[0], down)
@@ -582,11 +593,11 @@
     add_far(1, above, last_rows, down)
     kvg.push(7, dkv16.at[above], ynear.at[1], up)
     each([g], backward)
+    gg.finish()
+    mixed.stage3()
     for h in (0, 1):
         grads[:, h * 128 : (h + 1) * 128] = (dqt[h] * SCALE).T.astype(BF16)
-    gg.finish()
     join_cores(0, g)
-    mixed.stage4(mixed_out)
     kvg.arrive(6, ynear.at[0], up)
     kvg.arrive(7, ynear.at[1], down)
     grads[:, 256:512] = (
@@ -595,16 +606,14 @@
 
     final = Scatter(place, gbuf, tfar, tnear, ts, tfs, tns)
 
-    def spread(slots):
-        for slot in slots:
-            gbuf[slot] = (
-                dot(grads[:, 0:256], wqt[span(slot), :], 1, 1)
-                + dot(grads[:, 256:512], head_weights(slot), 1, 0)
-            ).astype(BF16)
-
-    spread(early)
-    final.stage0()
-    spread(late)
+    def spread(slot):
+        gbuf[slot] = (
+            dot(grads[:, 0:256], wqt[span(slot), :], 1, 1)
+            + dot(grads[:, 256:512], head_weights(slot), 1, 0)
+        ).astype(BF16)
+
+    final.stage0(spread)
+    mixed.stage4(mixed_out)
     final.stage1()
     final.stage2()
     final.stage3()

time: 126 us -> 116 us (0.921)
  Pallas kernels: 122 us -> 112 us
    pallas_call x1, Pallas kernels: 122 us -> 112 us  [local(): pl.pallas_call(layer, out_shape=(jax.ShapeDtypeStruct((512, 256), BF16),...]
where the time goes in v4:
time: 116 us
  Pallas kernels  112 us (97%)
  local copies, waits for them, and re-layouts  3.34 us (3%)
    pallas_call x1, Pallas kernels, local(): pl.pallas_call(layer, out_shape=(jax.ShapeDtypeStruct((512, 256), BF16),...  112 us
    unnamed x2, local copies, waits for them, and re-layouts  3.34 us

profile of v4, /device:TPU:0, one launch (start us, length us, event | category | flops | bytes accessed | tf_op | source)
XLA Modules:
  0.0 115.8 jit_solution(14717387884666399625)
XLA Ops:
  0.6 111.8 %layer.1 = (bf16[512,256]{1,0:T(8,128)(2,1)}, bf16[512,256]{1,0:T(8,128)(2,1)}) custom-call(bf16[512,256]{1,0:T(8,128)(2,1)} %tok.1, bf16[4096,256]{1,0:T(8,128)(2,1)} %wq.1, bf16[64,4096]{1,0:T(8,128)(2,1)} %bitcast.2, bf16[64,4096]{1,0:T(8,128)(2,1)} %bitcast.3, bf16[256,4096]{1,0:T(8,128)(2,1)} %wo.1, bf16[512,256]{1,0:T(8,128)(2,1)} %og.1, s32[4]{0:T(128)} %lens.1, ...), custom_call_target="tpu_custom_call" | custom-call | tf_op jit(solution)/shard_map/layer/pallas_call | solution.py:630
  112.4 1.7 %copy.12 = bf16[512,256]{1,0:T(8,128)(2,1)} copy(bf16[512,256]{1,0:T(8,128)(2,1)} %get-tuple-element.4) | data formatting | bytes 524288
  114.1 1.7 %copy.13 = bf16[512,256]{1,0:T(8,128)(2,1)} copy(bf16[512,256]{1,0:T(8,128)(2,1)} %get-tuple-element.5) | data formatting | bytes 524288

commit v5 on v4

--- a/solution.py
+++ b/solution.py
@@ -36,7 +36,7 @@
 
 def greet(place):
     barrier = pltpu.get_barrier_semaphore()
-    others = [place.at(dx=1), place.at(dx=3), place.at(dz=1), place.at(dz=3)]
+    others = [place.at(dx=1), place.at(dx=2), place.at(dx=3), place.at(dz=1), place.at(dz=3)]
     others += [place.at(dy=1), place.at(dy=3), place.at(dcore=1)]
     for other in others:
         pl.semaphore_signal(barrier, inc=1, device_id=other, device_id_type=MESH)
@@ -310,6 +310,77 @@
             copy.wait_send()
 
 
+class LineGather:
+    def __init__(self, place, along_x, own, buf, send, recv):
+        self.links, self.own, self.buf = Links(send, recv), own, buf
+        self.next = lambda sign: place.at(dx=sign) if along_x else place.at(dz=sign)
+
+    def stage0(self):
+        for r in (0, 1):
+            for s in (1, -1):
+                rows = Gather.rows(r, None)
+                self.links.push(
+                    r * 4 + (s < 0), self.own.at[rows, :], self.buf.at[-s % 4, rows, :], self.next(s)
+                )
+
+    def stage1(self):
+        for r in (0, 1):
+            for part, s in ((0, 1), (1, -1)):
+                whole, rows = Gather.rows(r, None), Gather.rows(r, part)
+                self.links.arrive(r * 4 + (s < 0), self.buf.at[-s % 4, whole, :], self.next(-s))
+                self.links.push(
+                    r * 4 + 2 + part, self.buf.at[-s % 4, rows, :], self.buf.at[2, rows, :], self.next(s)
+                )
+
+    def stage2(self):
+        for r in (0, 1):
+            for part, s in ((0, 1), (1, -1)):
+                self.links.arrive(r * 4 + 2 + part, self.buf.at[2, Gather.rows(r, part), :], self.next(-s))
+
+
+class LineScatter:
+    def __init__(self, place, along_x, buf, far, near, send, recv):
+        self.links, self.buf, self.far, self.near = Links(send, recv), buf, far, near
+        self.next = lambda sign: place.at(dx=sign) if along_x else place.at(dz=sign)
+
+    def start(self):
+        for r in (0, 1):
+            for part, s in ((0, -1), (1, 1)):
+                self.links.push(
+                    r * 4 + part, self.buf.at[2, Gather.rows(r, part), :], self.far.at[r, part], self.next(s)
+                )
+
+    def pass_on(self):
+        for r in (0, 1):
+            for part, s in ((0, -1), (1, 1)):
+                whole, rows = Gather.rows(r, None), Gather.rows(r, part)
+                self.links.arrive(r * 4 + part, self.far.at[r, part], self.next(-s))
+                self.buf[s % 4, rows, :] = (
+                    self.buf[s % 4, rows, :].astype(F32) + self.far[r, part].astype(F32)
+                ).astype(BF16)
+                self.links.push(
+                    r * 4 + 2 + part, self.buf.at[s % 4, whole, :], self.near.at[r, part], self.next(s)
+                )
+
+    def total(self, out):
+        for r in (0, 1):
+            rows = Gather.rows(r, None)
+            for part, s in ((0, -1), (1, 1)):
+                self.links.arrive(r * 4 + 2 + part, self.near.at[r, part], self.next(-s))
+            out[rows, :] = (
+                self.buf[0, rows, :].astype(F32)
+                + self.near[r, 0].astype(F32)
+                + self.near[r, 1].astype(F32)
+            ).astype(out.dtype)
+
+
+LINE_BUFS = [
+    pltpu.VMEM((4, 512, 256), BF16),
+    pltpu.VMEM((2, 2, 128, 256), BF16),
+    pltpu.VMEM((2, 2, 256, 256), BF16),
+]
+LINE_SEMS = [pltpu.SemaphoreType.DMA((8,))] * 4
+
 LINK_SEMS = [pltpu.SemaphoreType.DMA((16,)), pltpu.SemaphoreType.DMA((16,))]
 
 
@@ -326,10 +397,12 @@
 
 def layer(
     tok, wq, wk, wv, wo, og, lens, firsts, mixed_out, grad_out,
-    xbuf, gbuf, wqt, wkv, wot, acc, kacc, hacc,
-    qs, kvall, logits, probs, peak, sums, outs, att, dos, dlt, dqt, dkv16, core_in,
-    yfar, ynear, grads, mfar, mnear, tfar, tnear,
-    xs, xr, gs, gr, ms, mfs, mns, ts, tfs, tns, ws, wr, ks, kr, ds_, dr, lsem,
+    xbuf, wqt, wkv, wob, acc, kacc, hacc,
+    qs, kvall, logits, probs, peak, sums, outs, dos, dlt, dqt, dkv16, core_in,
+    yfar, ynear, grads, tfar, tnear,
+    gz, hp, hfar, hnear, ax, mp, mfar, mnear,
+    xs, xr, ts, tfs, tns, ws, wr, ks, kr, ds_, dr, os_, or_,
+    gs, gr, hs, hr, as_, ar, ms, mr, lsem,
 ):
     place = Place()
     g = place.g
@@ -341,14 +414,22 @@
         pltpu.make_async_copy(wv, wkv.at[1, own_rows, :], lsem.at[2]),
         pltpu.make_async_copy(tok, xbuf.at[0], lsem.at[0]),
         pltpu.make_async_copy(wq, wqt, lsem.at[3]),
-        pltpu.make_async_copy(og, gbuf.at[0], lsem.at[4]),
-        pltpu.make_async_copy(wo, wot, lsem.at[5]),
+        pltpu.make_async_copy(og, gz.at[0], lsem.at[4]),
     ]
+
+    def columns_of(dz, dx):
+        return pl.ds(pl.multiple_of(place.tensor(dz, dx) * 256, 256), 256)
+
+    for dz in range(4):
+        loads.append(pltpu.make_async_copy(wo.at[:, columns_of(dz, 0)], wob.at[0, dz], lsem.at[5 + dz]))
     for load in loads:
         load.start()
     greet(place)
     xg = Gather(place, tok, xbuf, xs, xr)
-    gg = Gather(place, og, gbuf, gs, gr)
+    gg = LineGather(place, False, og, gz, gs, gr)
+    head_sum = LineScatter(place, True, hp, hfar, hnear, hs, hr)
+    ag = LineGather(place, True, ax.at[0], ax, as_, ar)
+    mixed = LineScatter(place, False, mp, mfar, mnear, ms, mr)
     xg.stage0()
 
     def group_at(dy, dcore=0):
@@ -369,6 +450,53 @@
     loads[0].wait()
     loads[1].wait()
     wl.push(0, slice_of(own_rows, g), slice_of(own_rows, g), partner)
+
+    ol = Links(os_, or_)
+    own_slice = pl.ds(pl.multiple_of(g * 32, 32), 32)
+    for d in (1, 3, 2):
+        for dz in range(4):
+            ol.push(
+                (d - 1) * 4 + dz,
+                wo.at[own_slice, columns_of(dz, d)],
+                wob.at[4 - d, dz, own_slice, :],
+                place.at(dx=d),
+            )
+
+    def out_slice(group, part=None):
+        if part is None:
+            rows = pl.ds(pl.multiple_of(group * 32, 32), 32)
+        else:
+            rows = pl.ds(pl.multiple_of(group * 32 + part * 16, 16), 16)
+        return wob.at[pl.ds(1, 3), pl.ds(0, 4), rows, :]
+
+    def out_one():
+        for d in (1, 3, 2):
+            for dz in range(4):
+                ol.arrive((d - 1) * 4 + dz, wob.at[4 - d, dz, own_slice, :], place.at(dx=4 - d))
+        ref = out_slice(g)
+        ol.push(12, ref, ref, up)
+        ol.push(13, ref, ref, down)
+        ol.push(20, ref, ref, sibling)
+
+    def out_two():
+        ref = out_slice(below)
+        ol.arrive(12, ref, down)
+        ol.push(14, out_slice(below, 0), out_slice(below, 0), up)
+        ol.push(21, ref, ref, sibling)
+        ref = out_slice(above)
+        ol.arrive(13, ref, up)
+        ol.push(15, out_slice(above, 1), out_slice(above, 1), down)
+        ol.push(22, ref, ref, sibling)
+
+    def out_three():
+        ol.arrive(14, out_slice(across, 0), down)
+        ol.arrive(15, out_slice(across, 1), up)
+        ref = out_slice(across)
+        ol.push(23, ref, ref, sibling)
+
+    def out_four():
+        for index, group in ((20, sib_own), (21, sib_below), (22, sib_above), (23, sib_across)):
+            ol.arrive(index, out_slice(group), sibling)
 
     def weights_one():
         ref = slice_of(other_rows, g)
@@ -428,20 +556,33 @@
     def project_kv(pairs, first=False):
         gathered(kacc, xbuf, head_weights, 1, pairs, first)
 
-    def cotangent(pairs, first=False):
-        gathered(hacc, gbuf, lambda slot: wot[:, span(slot)], 1, pairs, first)
+    def head_part(dx):
+        total = dot(gz[0], wob[dx, 0], 1, 1)
+        for dz in (1, 2, 3):
+            total = total + dot(gz[dz], wob[dx, dz], 1, 1)
+        hp[dx] = total.astype(BF16)
+
+    def mixed_part(dz):
+        total = dot(ax[0], wob[0, dz])
+        for dx in (1, 2, 3):
+            total = total + dot(ax[dx], wob[dx, dz])
+        mp[dz] = total.astype(BF16)
 
     project(READY[0], True)
     xg.stage1()
+    gg.stage0()
     weights_one()
+    out_one()
     project(READY[1])
     xg.stage2a()
     xg.stage2b()
     weights_two()
+    out_two()
     project(READY[2])
     xg.stage3()
-    gg.stage0()
+    gg.stage1()
     weights_three()
+    out_three()
     project(READY[3])
     weights_four()
     project_kv(READY[0], True)
@@ -459,8 +600,8 @@
     project(READY[4])
     qs[0] = acc[:, 0:128].astype(BF16)
     qs[1] = acc[:, 128:256].astype(BF16)
-    loads[4].wait()
-    loads[5].wait()
+    for load in loads[4:]:
+        load.wait()
 
     lane = lax.broadcasted_iota(jnp.int32, (1, 512), 1)
     position = lane + g * 512
@@ -497,10 +638,12 @@
         return 0
 
     each([g], score)
-    gg.stage1()
-    cotangent(READY[0], True)
-    gg.stage2a()
-    cotangent(READY[1])
+    out_four()
+    gg.stage2()
+    head_part(2)
+    head_sum.start()
+    for dx in (1, 3, 0):
+        head_part(dx)
     kv.arrive(1, kvall.at[below], down)
     kv.push(3, kvall.at[below, first_rows, :], kvall.at[below, first_rows, :], up)
     kv.push(9, kvall.at[below], kvall.at[below], sibling)
@@ -509,14 +652,13 @@
     kv.push(10, kvall.at[above], kvall.at[above], sibling)
     kv.arrive(8, kvall.at[sib_own], sibling)
     each([sib_own, below, above], score)
-    gg.stage2b()
+    head_sum.pass_on()
     kv.arrive(3, kvall.at[across, first_rows, :], down)
     kv.arrive(4, kvall.at[across, last_rows, :], up)
     kv.push(11, kvall.at[across], kvall.at[across], sibling)
     kv.arrive(9, kvall.at[sib_below], sibling)
     kv.arrive(10, kvall.at[sib_above], sibling)
     each([sib_below, sib_above, across], score)
-    gg.stage3()
     kv.arrive(11, kvall.at[sib_across], sibling)
     each([sib_across], score)
     lax.fori_loop(0, g + 1, weigh, 0)
@@ -525,20 +667,10 @@
         inverse = 1.0 / sums[h]
         sums[h] = inverse
         outs[h] = outs[h] * inverse
-        att[:, h * 128 : (h + 1) * 128] = outs[h].T.astype(BF16)
-
-    xg.finish()
-    mixed = Scatter(place, xbuf, mfar, mnear, ms, mfs, mns)
-
-    def mix(slot):
-        xbuf[slot] = dot(att[...], wot[:, span(slot)]).astype(BF16)
-
-    mixed.stage0(mix)
-    cotangent(READY[2])
-    cotangent(READY[3])
-    gg.stage4()
-    cotangent(READY[4])
-
+        ax[0, :, h * 128 : (h + 1) * 128] = outs[h].T.astype(BF16)
+
+    ag.stage0()
+    head_sum.total(hacc)
     for h in (0, 1):
         grad_t = hacc[:, h * 128 : (h + 1) * 128].T * sums[h]
         out_t = outs[h].astype(BF16).astype(F32)
@@ -576,15 +708,13 @@
 
     each([sib_across, across], backward)
     to_sibling(2, sib_across)
-    mixed.stage1()
     join_cores(2, across)
     kvg.push(4, dkv16.at[across, first_rows, :], yfar.at[0], down)
     kvg.push(5, dkv16.at[across, last_rows, :], yfar.at[1], up)
-    each([sib_below, sib_above, sib_own], backward)
+    ag.stage1()
+    each([sib_below, sib_above], backward)
     to_sibling(3, sib_below)
     to_sibling(1, sib_above)
-    to_sibling(0, sib_own)
-    mixed.stage2()
     each([below, above], backward)
     join_cores(3, below)
     add_far(0, below, first_rows, up)
@@ -592,9 +722,16 @@
     join_cores(1, above)
     add_far(1, above, last_rows, down)
     kvg.push(7, dkv16.at[above], ynear.at[1], up)
+    ag.stage2()
+    mixed_part(2)
+    mixed.start()
+    each([sib_own], backward)
+    to_sibling(0, sib_own)
     each([g], backward)
-    gg.finish()
-    mixed.stage3()
+    for dz in (1, 3, 0):
+        mixed_part(dz)
+    mixed.pass_on()
+    xg.finish()
     for h in (0, 1):
         grads[:, h * 128 : (h + 1) * 128] = (dqt[h] * SCALE).T.astype(BF16)
     join_cores(0, g)
@@ -604,25 +741,22 @@
         dkv16[g].astype(F32) + ynear[0].astype(F32) + ynear[1].astype(F32)
     ).astype(BF16)
 
-    final = Scatter(place, gbuf, tfar, tnear, ts, tfs, tns)
+    final = Scatter(place, xbuf, tfar, tnear, ts, tfs, tns)
 
     def spread(slot):
-        gbuf[slot] = (
+        xbuf[slot] = (
             dot(grads[:, 0:256], wqt[span(slot), :], 1, 1)
             + dot(grads[:, 256:512], head_weights(slot), 1, 0)
         ).astype(BF16)
 
     final.stage0(spread)
-    mixed.stage4(mixed_out)
+    mixed.total(mixed_out)
     final.stage1()
     final.stage2()
     final.stage3()
     final.stage4(grad_out)
-    wl.finish()
-    kv.finish()
-    kvg.finish()
-    mixed.finish()
-    final.finish()
+    for links in (wl, ol, kv, kvg, gg.links, head_sum.links, ag.links, mixed.links, final):
+        links.finish()
 
 
 def local(tokens, w_query, w_key, w_value, w_out, out_grad, lengths, kv_first):
@@ -638,10 +772,9 @@
             out_specs=[pl.BlockSpec(memory_space=pltpu.VMEM)] * 2,
             scratch_shapes=[
                 pltpu.VMEM((16, 512, 256), BF16),
-                pltpu.VMEM((16, 512, 256), BF16),
                 pltpu.VMEM((4096, 256), BF16),
                 pltpu.VMEM((2, 128, 4096), BF16),
-                pltpu.VMEM((256, 4096), BF16),
+                pltpu.VMEM((4, 4, 256, 256), BF16),
                 pltpu.VMEM((512, 256), F32),
                 pltpu.VMEM((512, 256), F32),
                 pltpu.VMEM((512, 256), F32),
@@ -652,7 +785,6 @@
                 pltpu.VMEM((2, 1, 512), F32),
                 pltpu.VMEM((2, 1, 512), F32),
                 pltpu.VMEM((2, 128, 512), F32),
-                pltpu.VMEM((512, 256), BF16),
                 pltpu.VMEM((2, 512, 128), BF16),
                 pltpu.VMEM((2, 1, 512), F32),
                 pltpu.VMEM((2, 128, 512), F32),
@@ -662,15 +794,20 @@
                 pltpu.VMEM((2, 512, 256), BF16),
                 pltpu.VMEM((512, 512), BF16),
                 *SCATTER_BUFS,
-                *SCATTER_BUFS,
+                pltpu.VMEM((4, 512, 256), BF16),
+                *LINE_BUFS,
+                pltpu.VMEM((4, 512, 256), BF16),
+                *LINE_BUFS,
                 *GATHER_SEMS,
-                *GATHER_SEMS,
-                *SCATTER_SEMS,
                 *SCATTER_SEMS,
                 *LINK_SEMS,
                 *LINK_SEMS,
                 *LINK_SEMS,
-                pltpu.SemaphoreType.DMA((6,)),
+                pltpu.SemaphoreType.DMA((24,)),
+                pltpu.SemaphoreType.DMA((24,)),
+                *LINE_SEMS,
+                *LINE_SEMS,
+                pltpu.SemaphoreType.DMA((9,)),
             ],
             compiler_params=pltpu.CompilerParams(
                 collective_id=0, has_side_effects=True, vmem_limit_bytes=62 * 1024 * 1024

time: 116 us -> 113 us (0.974); the launches traced: 116 us -> 112 us
  Pallas kernels: 112 us -> 108 us
    pallas_call x1, Pallas kernels: 112 us -> 108 us  [local(): pl.pallas_call(layer, out_shape=(jax.ShapeDtypeStruct((512, 256), BF16),...]
where the time goes in v5:
time: 113 us; the launch traced here: 112 us
  Pallas kernels  108 us (96%)
  local copies, waits for them, and re-layouts  3.34 us (3%)
    pallas_call x1, Pallas kernels, local(): pl.pallas_call(layer, out_shape=(jax.ShapeDtypeStruct((512, 256), BF16),...  108 us
    unnamed x2, local copies, waits for them, and re-layouts  3.34 us

profile of v5, /device:TPU:0, one launch (start us, length us, event | category | flops | bytes accessed | tf_op | source)
XLA Modules:
  0.0 111.6 jit_solution(5944059505114708582)
XLA Ops:
  0.6 107.6 %layer.1 = (bf16[512,256]{1,0:T(8,128)(2,1)}, bf16[512,256]{1,0:T(8,128)(2,1)}) custom-call(bf16[512,256]{1,0:T(8,128)(2,1)} %tok.1, bf16[4096,256]{1,0:T(8,128)(2,1)} %wq.1, bf16[64,4096]{1,0:T(8,128)(2,1)} %bitcast.2, bf16[64,4096]{1,0:T(8,128)(2,1)} %bitcast.3, bf16[256,4096]{1,0:T(8,128)(2,1)} %wo.1, bf16[512,256]{1,0:T(8,128)(2,1)} %og.1, s32[4]{0:T(128)} %lens.1, ...), custom_call_target="tpu_custom_call" | custom-call | tf_op jit(solution)/shard_map/layer/pallas_call | solution.py:764
  108.2 1.7 %copy.12 = bf16[512,256]{1,0:T(8,128)(2,1)} copy(bf16[512,256]{1,0:T(8,128)(2,1)} %get-tuple-element.4) | data formatting | bytes 524288
  109.9 1.7 %copy.13 = bf16[512,256]{1,0:T(8,128)(2,1)} copy(bf16[512,256]{1,0:T(8,128)(2,1)} %get-tuple-element.5) | data formatting | bytes 524288

commit v6 on v5

--- a/solution.py
+++ b/solution.py
@@ -323,8 +323,8 @@
                     r * 4 + (s < 0), self.own.at[rows, :], self.buf.at[-s % 4, rows, :], self.next(s)
                 )
 
-    def stage1(self):
-        for r in (0, 1):
+    def stage1(self, halves=(0, 1)):
+        for r in halves:
             for part, s in ((0, 1), (1, -1)):
                 whole, rows = Gather.rows(r, None), Gather.rows(r, part)
                 self.links.arrive(r * 4 + (s < 0), self.buf.at[-s % 4, whole, :], self.next(-s))
@@ -332,8 +332,8 @@
                     r * 4 + 2 + part, self.buf.at[-s % 4, rows, :], self.buf.at[2, rows, :], self.next(s)
                 )
 
-    def stage2(self):
-        for r in (0, 1):
+    def stage2(self, halves=(0, 1)):
+        for r in halves:
             for part, s in ((0, 1), (1, -1)):
                 self.links.arrive(r * 4 + 2 + part, self.buf.at[2, Gather.rows(r, part), :], self.next(-s))
 
@@ -343,15 +343,15 @@
         self.links, self.buf, self.far, self.near = Links(send, recv), buf, far, near
         self.next = lambda sign: place.at(dx=sign) if along_x else place.at(dz=sign)
 
-    def start(self):
-        for r in (0, 1):
+    def start(self, halves=(0, 1)):
+        for r in halves:
             for part, s in ((0, -1), (1, 1)):
                 self.links.push(
                     r * 4 + part, self.buf.at[2, Gather.rows(r, part), :], self.far.at[r, part], self.next(s)
                 )
 
-    def pass_on(self):
-        for r in (0, 1):
+    def pass_on(self, halves=(0, 1)):
+        for r in halves:
             for part, s in ((0, -1), (1, 1)):
                 whole, rows = Gather.rows(r, None), Gather.rows(r, part)
                 self.links.arrive(r * 4 + part, self.far.at[r, part], self.next(-s))
@@ -398,7 +398,7 @@
 def layer(
     tok, wq, wk, wv, wo, og, lens, firsts, mixed_out, grad_out,
     xbuf, wqt, wkv, wob, acc, kacc, hacc,
-    qs, kvall, logits, probs, peak, sums, outs, dos, dlt, dqt, dkv16, core_in,
+    qs, kvall, logits, probs, peak, sums, outs, grad_t, dos, dlt, dqt, dkv16, core_in,
     yfar, ynear, grads, tfar, tnear,
     gz, hp, hfar, hnear, ax, mp, mfar, mnear,
     xs, xr, ts, tfs, tns, ws, wr, ks, kr, ds_, dr, os_, or_,
@@ -562,11 +562,12 @@
             total = total + dot(gz[dz], wob[dx, dz], 1, 1)
         hp[dx] = total.astype(BF16)
 
-    def mixed_part(dz):
-        total = dot(ax[0], wob[0, dz])
+    def mixed_part(dz, r):
+        rows = pl.ds(r * 256, 256)
+        total = dot(ax[0, rows, :], wob[0, dz])
         for dx in (1, 2, 3):
-            total = total + dot(ax[dx], wob[dx, dz])
-        mp[dz] = total.astype(BF16)
+            total = total + dot(ax[dx, rows, :], wob[dx, dz])
+        mp[dz, rows, :] = total.astype(BF16)
 
     project(READY[0], True)
     xg.stage1()
@@ -661,21 +662,19 @@
     each([sib_below, sib_above, across], score)
     kv.arrive(11, kvall.at[sib_across], sibling)
     each([sib_across], score)
-    lax.fori_loop(0, g + 1, weigh, 0)
+    lax.fori_loop(0, (g + 1) // 2, weigh, 0)
+    head_sum.total(hacc)
+    for h in (0, 1):
+        grad_t[h] = hacc[:, h * 128 : (h + 1) * 128].T
+    lax.fori_loop((g + 1) // 2, g + 1, weigh, 0)
 
     for h in (0, 1):
         inverse = 1.0 / sums[h]
-        sums[h] = inverse
         outs[h] = outs[h] * inverse
-        ax[0, :, h * 128 : (h + 1) * 128] = outs[h].T.astype(BF16)
-
-    ag.stage0()
-    head_sum.total(hacc)
-    for h in (0, 1):
-        grad_t = hacc[:, h * 128 : (h + 1) * 128].T * sums[h]
         out_t = outs[h].astype(BF16).astype(F32)
-        dlt[h] = jnp.sum(grad_t * out_t, axis=0, keepdims=True)
-        dos[h] = grad_t.T.astype(BF16)
+        dlt[h] = jnp.sum(grad_t[h] * out_t, axis=0, keepdims=True) * inverse
+        column = jnp.broadcast_to(inverse, (8, 512)).T[:, 0:1]
+        dos[h] = (hacc[:, h * 128 : (h + 1) * 128] * column).astype(BF16)
 
     def backward(k):
         @pl.when(k <= g)
@@ -706,31 +705,43 @@
         kvg.arrive(4 + part, yfar.at[part], source)
         dkv16[group, rows, :] = (dkv16[group, rows, :].astype(F32) + yfar[part].astype(F32)).astype(BF16)
 
-    each([sib_across, across], backward)
+    for h in (0, 1):
+        ax[0, :, h * 128 : (h + 1) * 128] = outs[h].T.astype(BF16)
+    ag.stage0()
+    each([sib_across], backward)
     to_sibling(2, sib_across)
+    each([across, sib_below], backward)
+    to_sibling(3, sib_below)
     join_cores(2, across)
     kvg.push(4, dkv16.at[across, first_rows, :], yfar.at[0], down)
     kvg.push(5, dkv16.at[across, last_rows, :], yfar.at[1], up)
-    ag.stage1()
-    each([sib_below, sib_above], backward)
-    to_sibling(3, sib_below)
+    ag.stage1((0,))
+    each([sib_above, below], backward)
     to_sibling(1, sib_above)
-    each([below, above], backward)
+    ag.stage1((1,))
     join_cores(3, below)
     add_far(0, below, first_rows, up)
     kvg.push(6, dkv16.at[below], ynear.at[0], down)
+    each([above], backward)
     join_cores(1, above)
     add_far(1, above, last_rows, down)
     kvg.push(7, dkv16.at[above], ynear.at[1], up)
-    ag.stage2()
-    mixed_part(2)
-    mixed.start()
+    ag.stage2((0,))
+    mixed_part(2, 0)
+    mixed.start((0,))
     each([sib_own], backward)
     to_sibling(0, sib_own)
+    ag.stage2((1,))
+    mixed_part(2, 1)
+    mixed.start((1,))
+    for r in (0, 1):
+        mixed_part(1, r)
+        mixed_part(3, r)
     each([g], backward)
-    for dz in (1, 3, 0):
-        mixed_part(dz)
-    mixed.pass_on()
+    mixed.pass_on((0,))
+    for r in (0, 1):
+        mixed_part(0, r)
+    mixed.pass_on((1,))
     xg.finish()
     for h in (0, 1):
         grads[:, h * 128 : (h + 1) * 128] = (dqt[h] * SCALE).T.astype(BF16)
@@ -759,9 +770,24 @@
         links.finish()
 
 
+def hand_on(mixed, grad):
+    def body(a, b, c, d):
+        c[...] = a[...]
+        d[...] = b[...]
+
+    spec = pl.BlockSpec((512, 256), lambda: (0, 0))
+    return pl.pallas_call(
+        body,
+        out_shape=(jax.ShapeDtypeStruct((512, 256), BF16),) * 2,
+        in_specs=[spec] * 2,
+        out_specs=[spec] * 2,
+        name="hand_on",
+    )(mixed, grad)
+
+
 def local(tokens, w_query, w_key, w_value, w_out, out_grad, lengths, kv_first):
-    return tuple(
-        pl.pallas_call(
+    return hand_on(
+        *pl.pallas_call(
             layer,
             out_shape=(
                 jax.ShapeDtypeStruct((512, 256), BF16),
@@ -784,6 +810,7 @@
                 pltpu.VMEM((8, 2, 512, 512), BF16),
                 pltpu.VMEM((2, 1, 512), F32),
                 pltpu.VMEM((2, 1, 512), F32),
+                pltpu.VMEM((2, 128, 512), F32),
                 pltpu.VMEM((2, 128, 512), F32),
                 pltpu.VMEM((2, 512, 128), BF16),
                 pltpu.VMEM((2, 1, 512), F32),

time: 113 us -> 109 us (0.965); the launches traced: 112 us -> 109 us
  local copies, waits for them, and re-layouts: 3.34 us -> 0 us
    unnamed x2 -> x0, local copies, waits for them, and re-layouts: 3.34 us -> none
    pallas_call x0 -> x1, Pallas kernels: none -> 1.84 us  [hand_on(): pl.pallas_call(body, out_shape=(jax.ShapeDtypeStruct((512, 256), BF16),)...]
    pallas_call x1, Pallas kernels: 108 us -> 106 us  [local(): pl.pallas_call(layer, out_shape=(jax.ShapeDtypeStruct((512, 256), BF16),...]
where the time goes in v6:
time: 109 us
  Pallas kernels  108 us (99%)
    pallas_call x1, Pallas kernels, local(): pl.pallas_call(layer, out_shape=(jax.ShapeDtypeStruct((512, 256), BF16),...  106 us

profile of v6, /device:TPU:0, one launch (start us, length us, event | category | flops | bytes accessed | tf_op | source)
XLA Modules:
  0.0 108.7 jit_solution(11675374219571449149)
XLA Ops:
  0.6 106.3 %layer.1 = (bf16[512,256]{1,0:T(8,128)(2,1)}, bf16[512,256]{1,0:T(8,128)(2,1)}) custom-call(bf16[512,256]{1,0:T(8,128)(2,1)} %tok.1, bf16[4096,256]{1,0:T(8,128)(2,1)} %wq.1, bf16[64,4096]{1,0:T(8,128)(2,1)} %bitcast.2, bf16[64,4096]{1,0:T(8,128)(2,1)} %bitcast.3, bf16[256,4096]{1,0:T(8,128)(2,1)} %wo.1, bf16[512,256]{1,0:T(8,128)(2,1)} %og.1, s32[4]{0:T(128)} %lens.1, ...), custom_call_target="tpu_custom_call" | custom-call | tf_op jit(solution)/shard_map/layer/pallas_call | solution.py:790
  106.9 1.8 %hand_on.1 = (bf16[512,256]{1,0:T(8,128)(2,1)}, bf16[512,256]{1,0:T(8,128)(2,1)}) custom-call(bf16[512,256]{1,0:T(8,128)(2,1)} %get-tuple-element.4.a, bf16[512,256]{1,0:T(8,128)(2,1)} %get-tuple-element.5.b), custom_call_target="tpu_custom_call" | custom-call | tf_op jit(solution)/shard_map/hand_on/pallas_call | solution.py:779

commit v7 on v6

--- a/solution.py
+++ b/solution.py
@@ -737,8 +737,8 @@
     for r in (0, 1):
         mixed_part(1, r)
         mixed_part(3, r)
+    mixed.pass_on((0,))
     each([g], backward)
-    mixed.pass_on((0,))
     for r in (0, 1):
         mixed_part(0, r)
     mixed.pass_on((1,))

time: 109 us -> 108 us (level)
    pallas_call x1, Pallas kernels: 106 us -> 105 us  [local(): pl.pallas_call(layer, out_shape=(jax.ShapeDtypeStruct((512, 256), BF16),...]
where the time goes in v7:
time: 108 us
  Pallas kernels  107 us (99%)
    pallas_call x1, Pallas kernels, local(): pl.pallas_call(layer, out_shape=(jax.ShapeDtypeStruct((512, 256), BF16),...  105 us

profile of v7, /device:TPU:0, one launch (start us, length us, event | category | flops | bytes accessed | tf_op | source)
XLA Modules:
  0.0 107.6 jit_solution(2134400016696850227)
XLA Ops:
  0.6 105.2 %layer.1 = (bf16[512,256]{1,0:T(8,128)(2,1)}, bf16[512,256]{1,0:T(8,128)(2,1)}) custom-call(bf16[512,256]{1,0:T(8,128)(2,1)} %tok.1, bf16[4096,256]{1,0:T(8,128)(2,1)} %wq.1, bf16[64,4096]{1,0:T(8,128)(2,1)} %bitcast.2, bf16[64,4096]{1,0:T(8,128)(2,1)} %bitcast.3, bf16[256,4096]{1,0:T(8,128)(2,1)} %wo.1, bf16[512,256]{1,0:T(8,128)(2,1)} %og.1, s32[4]{0:T(128)} %lens.1, ...), custom_call_target="tpu_custom_call" | custom-call | tf_op jit(solution)/shard_map/layer/pallas_call | solution.py:790
  105.8 1.8 %hand_on.1 = (bf16[512,256]{1,0:T(8,128)(2,1)}, bf16[512,256]{1,0:T(8,128)(2,1)}) custom-call(bf16[512,256]{1,0:T(8,128)(2,1)} %get-tuple-element.4.a, bf16[512,256]{1,0:T(8,128)(2,1)} %get-tuple-element.5.b), custom_call_target="tpu_custom_call" | custom-call | tf_op jit(solution)/shard_map/hand_on/pallas_call | solution.py:779

commit v8 on v7

--- a/solution.py
+++ b/solution.py
@@ -595,8 +595,11 @@
 
     kv = Links(ks, kr)
     kvall[g] = kacc[...].astype(BF16)
-    kv.push(1, kvall.at[g], kvall.at[g], up)
-    kv.push(2, kvall.at[g], kvall.at[g], down)
+    own_first, own_last = kvall.at[g, first_rows, :], kvall.at[g, last_rows, :]
+    kv.push(1, own_first, own_first, up)
+    kv.push(2, own_last, own_last, down)
+    kv.push(5, own_last, own_last, up)
+    kv.push(6, own_first, own_first, down)
     kv.push(8, kvall.at[g], kvall.at[g], sibling)
     project(READY[4])
     qs[0] = acc[:, 0:128].astype(BF16)
@@ -645,11 +648,13 @@
     head_sum.start()
     for dx in (1, 3, 0):
         head_part(dx)
-    kv.arrive(1, kvall.at[below], down)
+    kv.arrive(1, kvall.at[below, first_rows, :], down)
     kv.push(3, kvall.at[below, first_rows, :], kvall.at[below, first_rows, :], up)
+    kv.arrive(2, kvall.at[above, last_rows, :], up)
+    kv.push(4, kvall.at[above, last_rows, :], kvall.at[above, last_rows, :], down)
+    kv.arrive(5, kvall.at[below, last_rows, :], down)
     kv.push(9, kvall.at[below], kvall.at[below], sibling)
-    kv.arrive(2, kvall.at[above], up)
-    kv.push(4, kvall.at[above, last_rows, :], kvall.at[above, last_rows, :], down)
+    kv.arrive(6, kvall.at[above, first_rows, :], up)
     kv.push(10, kvall.at[above], kvall.at[above], sibling)
     kv.arrive(8, kvall.at[sib_own], sibling)
     each([sib_own, below, above], score)

time: 108 us -> 106 us (0.981)
  Pallas kernels: 107 us -> 105 us
    pallas_call x1, Pallas kernels: 105 us -> 104 us  [local(): pl.pallas_call(layer, out_shape=(jax.ShapeDtypeStruct((512, 256), BF16),...]
where the time goes in v8:
time: 106 us
  Pallas kernels  105 us (99%)
    pallas_call x1, Pallas kernels, local(): pl.pallas_call(layer, out_shape=(jax.ShapeDtypeStruct((512, 256), BF16),...  104 us

profile of v8, /device:TPU:0, one launch (start us, length us, event | category | flops | bytes accessed | tf_op | source)
XLA Modules:
  0.0 106.0 jit_solution(12154827572283034242)
XLA Ops:
  0.6 103.5 %layer.1 = (bf16[512,256]{1,0:T(8,128)(2,1)}, bf16[512,256]{1,0:T(8,128)(2,1)}) custom-call(bf16[512,256]{1,0:T(8,128)(2,1)} %tok.1, bf16[4096,256]{1,0:T(8,128)(2,1)} %wq.1, bf16[64,4096]{1,0:T(8,128)(2,1)} %bitcast.2, bf16[64,4096]{1,0:T(8,128)(2,1)} %bitcast.3, bf16[256,4096]{1,0:T(8,128)(2,1)} %wo.1, bf16[512,256]{1,0:T(8,128)(2,1)} %og.1, s32[4]{0:T(128)} %lens.1, ...), custom_call_target="tpu_custom_call" | custom-call | tf_op jit(solution)/shard_map/layer/pallas_call | solution.py:795
  104.2 1.8 %hand_on.1 = (bf16[512,256]{1,0:T(8,128)(2,1)}, bf16[512,256]{1,0:T(8,128)(2,1)}) custom-call(bf16[512,256]{1,0:T(8,128)(2,1)} %get-tuple-element.4.a, bf16[512,256]{1,0:T(8,128)(2,1)} %get-tuple-element.5.b), custom_call_target="tpu_custom_call" | custom-call | tf_op jit(solution)/shard_map/hand_on/pallas_call | solution.py:784
